TPU v7x, 256 devices: a whole 4x4x8 slice. The times are simulated.
256 devices in a mesh: row: 8 (over y, core), col: 8 (over z), layer: 4 (over x).
Axes of the slice: x: 4, y: 4, z: 8, core: 2. Of those that a mesh axis runs over, the one named last changes fastest.
Arguments:
- a_blocks: bfloat16 [1536, 128, 128], P(('row', 'col', 'layer')), may hold values from -6 to 6
- a_where: int32 [1536, 2], P(('row', 'col', 'layer')), may hold values from 0 to 63, as said below
- b_blocks: bfloat16 [2048, 128, 128], P(('row', 'col', 'layer')), may hold values from -0.375 to 0.375
- b_where: int32 [2048, 2], P(('row', 'col', 'layer')), may hold values from 0 to 63, as said below
Outputs:
- product: float32 [16384, 16384], P('row', ('col', 'layer'))
Inputs may be any that keep to these rules, and one draw needn't show every extreme that they name: For slot s on the device with grid coordinates (p, q, t): a_where[s, 1] = (m * (number of col devices) + q) * (number of layer devices) + t for some m below 2; a_where[s, 0] is a block row below 16, or 16 for an empty slot. No device holds the same (row, column) pair twice. At least a quarter of each device's slots are live, at positions drawn from the seed, and in every draw some device has all 6 slots live. For slot s on the device with grid coordinates (p, q, t): b_where[s, 0] is a block row k of B with k mod (number of row devices) = p; b_where[s, 1] is a local block column below 4, or 4 for an empty slot. No device holds the same pair twice. At least a quarter of each device's slots are live, at positions drawn from the seed, and in every draw some device has all 8 slots live.
All inputs are finite; a program needn't handle non-finite values.
Results may differ from a plain program's by a relative error of at most 0.0003.
Values may be sent and summed in bfloat16 or wider, within the bound.
No kernel may reach another device: no remote copies, remote signals or barrier semaphores. Data moves between devices by JAX's collectives and lax.ppermute only.
A program may use at most 128 MiB of HBM per device.

v0:
```python
import jax
import jax.numpy as jnp
from jax import lax
from jax.sharding import PartitionSpec as P

BS = 128
RB = 16
CS = 4
KD = 2


def pack_columns(blocks, where, total_k):
    count = blocks.shape[0]
    target = jnp.where(where[:, 1] < CS, where[:, 0] * CS + where[:, 1], -1)
    picker = (target[None, :] == jnp.arange(total_k * CS, dtype=jnp.int32)[:, None]).astype(
        jnp.bfloat16
    )
    flat = jnp.dot(
        picker, blocks.reshape(count, BS * BS), preferred_element_type=jnp.float32
    ).astype(jnp.bfloat16)
    flat = flat.reshape(total_k, CS, BS, BS).transpose(0, 2, 1, 3)
    return flat.reshape(total_k, BS, CS * BS)


def make_adder(dense):

    def adder(total, piece, start):
        blocks, where = piece
        count = blocks.shape[0]
        group = max((factor for factor in range(1, min(count, 64) + 1) if count % factor == 0))

        def one_group(acc, item):
            group_blocks, group_where = item
            strips = jnp.take(dense, group_where[:, 1], axis=0)
            partial_rows = jnp.einsum(
                "gab,gbc->gac", group_blocks, strips, preferred_element_type=jnp.float32
            )
            return (acc.at[group_where[:, 0]].add(partial_rows, mode="drop"), None)

        items = (
            blocks.reshape(count // group, group, BS, BS),
            where.reshape(count // group, group, 2),
        )
        total, unused = lax.scan(one_group, total, items)
        return total

    return adder


def body(a_blocks, a_where, b_blocks, b_where):
    total_k = KD * lax.axis_size("col") * lax.axis_size("layer")
    blocks_b, where_b = (
        lax.all_gather(b_blocks, "row", axis=0, tiled=True),
        lax.all_gather(b_where, "row", axis=0, tiled=True),
    )
    dense = pack_columns(blocks_b, where_b, total_k)
    adder = make_adder(dense)
    empty = jnp.zeros((RB, BS, CS * BS), jnp.float32)
    total = adder(
        empty,
        (
            lax.all_gather(a_blocks, ("col", "layer"), axis=0, tiled=True),
            lax.all_gather(a_where, ("col", "layer"), axis=0, tiled=True),
        ),
        jnp.int32(0),
    )
    return total.reshape(RB * BS, CS * BS)


def solution(mesh):
    in_specs = (
        P(("row", "col", "layer"), None, None),
        P(("row", "col", "layer"), None),
        P(("row", "col", "layer"), None, None),
        P(("row", "col", "layer"), None),
    )
    out_specs = P("row", ("col", "layer"))
    return jax.shard_map(body, mesh=mesh, in_specs=in_specs, out_specs=out_specs, check_vma=False)
```

profile of v0, /device:TPU:24, one launch (start us, length us, event | category | flops | bytes accessed | tf_op | source)
XLA Modules:
  0.0 308.4 jit_solution(1145207475288112660)
XLA Ops:
  6.5 0.0 all-gather.7.cloned.1.call-start
  6.5 0.7 all-gather.7.cloned.1.call-update
  7.3 0.0 all-gather.5.cloned.1.call-start
  7.3 0.7 all-gather.5.cloned.1.call-update
  8.0 8.8 %all-gather.1 = s32[8,8,2]{1,2,0:T(2,128)S(1)} all-gather(s32[1,8,2]{1,2,0:T(2,128)} %bitcast.50), channel_id=1, replica_groups=mesh['row'=8,'col'=8,'layer'=4] {'row'}, dimensions={0}, use_global_device_ids=true | all-gather | bytes 576 | tf_op jit(solution)/shard_map/all_gather | solution.py:54
  16.8 0.1 reshape.69
  16.9 44.8 %all-gather = s32[32,6,2]{1,2,0:T(2,128)S(1)} all-gather(s32[1,6,2]{1,2,0:T(2,128)} %bitcast.51), channel_id=1, replica_groups=mesh['row'=8,'col'=8,'layer'=4] {'col','layer'}, dimensions={0}, use_global_device_ids=true | all-gather | bytes 1584 | tf_op jit(solution)/shard_map/all_gather | solution.py:63
  61.7 0.1 reshape.44
  61.8 0.0 all-gather.7.cloned.1.call-done
  61.8 7.2 %fusion.10 = bf16[32,8,128,128]{3,1,2,0:T(8,128)(2,1)} fusion(bf16[8,8,128,128]{3,2,1,0:T(8,128)(2,1)} %bitcast.47, s32[64]{0:T(128)S(1)} %fusion.14), kind=kOutput, calls=%fused_computation.19 | convolution fusion | flops 541081600 | bytes 10486016 | tf_op jit(solution)/shard_map/dot_general | solution.py:18
  69.0 9.2 %copy.18 = bf16[32,8,128,128]{3,2,1,0:T(8,128)(2,1)} copy(bf16[32,8,128,128]{3,1,2,0:T(8,128)(2,1)} %fusion.10) | data formatting | bytes 16777216
  78.2 8.3 %copy.24 = bf16[64,4,16,8,128]{4,3,1,2,0:T(8,128)(2,1)} copy(bf16[64,4,16,8,128]{4,3,2,1,0:T(8,128)(2,1)} %bitcast.45) | data formatting | bytes 16777216 | tf_op jit(solution)/shard_map/reshape | solution.py:22
  86.5 44.8 %all-gather.5.cloned.1.call-done = bf16[192,128,128]{2,1,0:T(8,128)(2,1)} async-done(((bf16[6,128,128]{2,1,0:T(8,128)(2,1)}), bf16[192,128,128]{2,1,0:T(8,128)(2,1)}) %all-gather.5.cloned.1.call-update) | async-done | bytes 6291472 | tf_op jit(solution)/shard_map/all_gather | solution.py:62
  131.3 2.5 broadcast_in_dim.20
  133.8 167.7 %while.10 = (s32[]{:T(128)}, f32[16,128,512]{2,1,0:T(8,128)}, s32[3,64,2]{1,0,2:T(4,128)S(1)}, bf16[3,64,128,128]{3,2,1,0:T(8,128)(2,1)}, bf16[64,128,512]{2,1,0:T(8,128)(2,1)}, /*index=5*/s32[]{:T(128)}) while((s32[]{:T(128)}, f32[16,128,512]{2,1,0:T(8,128)}, s32[3,64,2]{1,0,2:T(4,128)S(1)}, bf16[3,64,128,128]{3,2,1,0:T(8,128)(2,1)}, ...), condition=%wide.region_2.3_spmd, body=%wide.region_0.2_spmd.sunk | while | flops 1082132224 | bytes 94379720 | solution.py:44
  133.9 8.9 %gather_fusion = bf16[64,128,512]{2,1,0:T(8,128)(2,1)} fusion(bf16[64,128,512]{2,1,0:T(8,128)(2,1)} %get-tuple-element.106, s32[1024]{0:T(1024)S(1)} %pad_clamp_fusion.2), kind=kCustom, calls=%fused_computation.clone.1 | custom fusion | bytes 16777472 | tf_op jit(solution)/shard_map/while/body/eval_jaxpr/jit(_take)/gather | solution.py:34
  142.8 12.2 %fusion.22 = f32[64,128,512]{2,1,0:T(8,128)} fusion(bf16[64,128,512]{2,1,0:T(8,128)(2,1)} %gather_fusion, pred[64]{0:T(512)(128)(4,1)S(1)} %and_bitcast_fusion.2, bf16[3,64,128,128]{3,2,1,0:T(8,128)(2,1)} %get-tuple-element.105, s32[]{:T(128)} %get-tuple-element.96), kind=kOutput, calls=%fused_computation.2.clone.1 | convolution fusion | flops 1077936128 | bytes 27263552 | tf_op jit(solution)/shard_map/while/body/eval_jaxpr/gab,gbc->gac/dot_general | solution.py:35
  154.9 34.9 %scatter_fusion = f32[16,128,512]{2,1,0:T(8,128)} fusion(f32[16,128,512]{2,1,0:T(8,128)} %get-tuple-element.97, s32[64]{0:T(128)S(1)} %get-tuple-element.88, f32[64,128,512]{2,1,0:T(8,128)} %fusion.22), kind=kCustom, calls=%fused_computation.1.clone.1 | custom fusion | flops 4194304 | bytes 50331904 | tf_op jit(solution)/shard_map/while/body/eval_jaxpr/scatter-add | solution.py:38
  189.9 8.9 %gather_fusion = bf16[64,128,512]{2,1,0:T(8,128)(2,1)} fusion(bf16[64,128,512]{2,1,0:T(8,128)(2,1)} %get-tuple-element.106, s32[1024]{0:T(1024)S(1)} %pad_clamp_fusion.2), kind=kCustom, calls=%fused_computation.clone.1 | custom fusion | bytes 16777472 | tf_op jit(solution)/shard_map/while/body/eval_jaxpr/jit(_take)/gather | solution.py:34
  198.8 12.2 %fusion.22 = f32[64,128,512]{2,1,0:T(8,128)} fusion(bf16[64,128,512]{2,1,0:T(8,128)(2,1)} %gather_fusion, pred[64]{0:T(512)(128)(4,1)S(1)} %and_bitcast_fusion.2, bf16[3,64,128,128]{3,2,1,0:T(8,128)(2,1)} %get-tuple-element.105, s32[]{:T(128)} %get-tuple-element.96), kind=kOutput, calls=%fused_computation.2.clone.1 | convolution fusion | flops 1077936128 | bytes 27263552 | tf_op jit(solution)/shard_map/while/body/eval_jaxpr/gab,gbc->gac/dot_general | solution.py:35
  211.0 34.7 %scatter_fusion = f32[16,128,512]{2,1,0:T(8,128)} fusion(f32[16,128,512]{2,1,0:T(8,128)} %get-tuple-element.97, s32[64]{0:T(128)S(1)} %get-tuple-element.88, f32[64,128,512]{2,1,0:T(8,128)} %fusion.22), kind=kCustom, calls=%fused_computation.1.clone.1 | custom fusion | flops 4194304 | bytes 50331904 | tf_op jit(solution)/shard_map/while/body/eval_jaxpr/scatter-add | solution.py:38
  245.7 8.9 %gather_fusion = bf16[64,128,512]{2,1,0:T(8,128)(2,1)} fusion(bf16[64,128,512]{2,1,0:T(8,128)(2,1)} %get-tuple-element.106, s32[1024]{0:T(1024)S(1)} %pad_clamp_fusion.2), kind=kCustom, calls=%fused_computation.clone.1 | custom fusion | bytes 16777472 | tf_op jit(solution)/shard_map/while/body/eval_jaxpr/jit(_take)/gather | solution.py:34
  254.6 12.2 %fusion.22 = f32[64,128,512]{2,1,0:T(8,128)} fusion(bf16[64,128,512]{2,1,0:T(8,128)(2,1)} %gather_fusion, pred[64]{0:T(512)(128)(4,1)S(1)} %and_bitcast_fusion.2, bf16[3,64,128,128]{3,2,1,0:T(8,128)(2,1)} %get-tuple-element.105, s32[]{:T(128)} %get-tuple-element.96), kind=kOutput, calls=%fused_computation.2.clone.1 | convolution fusion | flops 1077936128 | bytes 27263552 | tf_op jit(solution)/shard_map/while/body/eval_jaxpr/gab,gbc->gac/dot_general | solution.py:35
  266.8 34.8 %scatter_fusion = f32[16,128,512]{2,1,0:T(8,128)} fusion(f32[16,128,512]{2,1,0:T(8,128)} %get-tuple-element.97, s32[64]{0:T(128)S(1)} %get-tuple-element.88, f32[64,128,512]{2,1,0:T(8,128)} %fusion.22), kind=kCustom, calls=%fused_computation.1.clone.1 | custom fusion | flops 4194304 | bytes 50331904 | tf_op jit(solution)/shard_map/while/body/eval_jaxpr/scatter-add | solution.py:38
  (15 shorter events, 0.1 us)
Async XLA Ops:
  6.5 55.3 %all-gather.7.cloned.1.call-start = ((), (), s32[]{:S(2)}) async-start(), calls=%async_computation.1 | async-start | bytes 2359296 | tf_op jit(solution)/shard_map/all_gather | solution.py:53
  7.3 124.0 %all-gather.5.cloned.1.call-start = ((), (), s32[]{:S(2)}) async-start(), calls=%async_computation | async-start | bytes 6488064 | tf_op jit(solution)/shard_map/all_gather | solution.py:62
Sparse Core Ops, SparseCore 0:
  9.2 29.4 all-gather.6
  41.3 89.9 all-gather.4
where the time goes:
time: 311 us; the launch traced here: 308 us
  other arithmetic  105 us (34%)
  blocking collectives  53.6 us (17%)
  local copies, waits for them, and re-layouts  46.9 us (15%)
  waiting for transfers between devices  46.2 us (15%)
  matrix products  43.7 us (14%)
  between operations  13.4 us (4%)
    scatter-add x3, other arithmetic, one_group(): return (acc.at[group_where[:, 0]].add(partial_rows, mode='drop'), None)  104 us
    all_gather x1, waiting for transfers between devices, body(): lax.all_gather(a_blocks, ('col', 'layer'), axis=0, tiled=True)  44.8 us
    all_gather x1, blocking collectives, body(): lax.all_gather(a_where, ('col', 'layer'), axis=0, tiled=True)  44.8 us
    dot_general x3, matrix products, one_group(): jnp.einsum('gab,gbc->gac', group_blocks, strips, preferred_element_type=j...  36.5 us
    gather x3, local copies, waits for them, and re-layouts, one_group(): strips = jnp.take(dense, group_where[:, 1], axis=0)  26.7 us
    unnamed x2, local copies, waits for them, and re-layouts  9.29 us
    all_gather x1, blocking collectives, body(): lax.all_gather(b_where, 'row', axis=0, tiled=True)  8.79 us
    reshape x1, local copies, waits for them, and re-layouts, pack_columns(): return flat.reshape(total_k, BS, CS * BS)  8.25 us
  transfers between devices with their start and end apart: 2, of which 1 were waited for; matrix products, arithmetic and copies ran while one was open for 8% of the time, Pallas kernels for 0%

commit v1 on v0

v1 whole, which is shorter than its diff:
```python
import jax
import jax.numpy as jnp
import numpy as np
from jax import lax
from jax.experimental import pallas as pl
from jax.experimental.pallas import tpu as pltpu
from jax.sharding import PartitionSpec as P

BS = 128
RB = 16
CS = 4
SA = 6
SB = 8
NZ = 8
NX = 4
NY = 4
INFO = 16
CUT = 448
UR = INFO + CUT
VR = SA * BS - CUT
BR = INFO + SB * BS
CHUNKS = NZ * NX
PARTS = NY * 2
GROUP = 8
LIST = CHUNKS * SA * CS + 2 * GROUP
KMAX = 64

Z_ORDER = (0, 1, -1, 2, -2, 3, -3, 4)
X_ORDER = (0, 1, -1, 2)
U_ORDER = [(dz, dx) for dx in X_ORDER for dz in Z_ORDER]
V_ORDER = [(dz, dx) for dz in Z_ORDER for dx in X_ORDER]


def cat(pieces):
    return jnp.concatenate(pieces, axis=0)


def tie(*arrays):
    return lax.optimization_barrier(arrays)


def along_z(x, d):
    return lax.ppermute(x, "col", [(i, (i + d) % NZ) for i in range(NZ)])


def along_x(x, d):
    return lax.ppermute(x, "layer", [(i, (i + d) % NX) for i in range(NX)])


def along_y(x, d):
    n = 2 * NY
    return lax.ppermute(x, "row", [(i, (i + 2 * d) % n) for i in range(n)])


def other_core(x):
    return lax.ppermute(x, "row", [(i, i ^ 1) for i in range(2 * NY)])


def with_info(first, second, blocks):
    n = first.shape[0]
    row = jnp.concatenate([first, second]).astype(jnp.bfloat16)
    tile = jnp.zeros((INFO, BS), jnp.bfloat16).at[0, : 2 * n].set(row)
    return cat([tile, blocks])


def kernel(tab, a_ref, b_ref, o_hbm, out, mid, bslot, work, work_mid, info, sinfo, sem):
    for i in range(CHUNKS):
        info[i : i + 1, :] = a_ref[i * UR : i * UR + INFO, :][0:1].astype(jnp.float32).astype(jnp.int32)
    for i in range(PARTS):
        info[CHUNKS + i : CHUNKS + i + 1, :] = (
            b_ref[i * BR : i * BR + INFO, :][0:1].astype(jnp.float32).astype(jnp.int32)
        )
    to_scalar = pltpu.make_async_copy(info, sinfo, sem.at[0])
    to_scalar.start()

    def clear(i, carry):
        out[i] = jnp.zeros((BS, CS * BS), jnp.float32)
        return carry

    lax.fori_loop(0, RB + 1, clear, 0)

    def join(i, carry):
        top = pl.multiple_of(i * UR + INFO + CUT // BS * BS, 16)
        low = pl.multiple_of(tab[1, i], 16)
        mid[pl.ds(pl.multiple_of(i * BS, BS), CUT % BS), :] = a_ref[pl.ds(top, CUT % BS), :]
        mid[pl.ds(pl.multiple_of(i * BS + CUT % BS, 16), BS - CUT % BS), :] = a_ref[pl.ds(low, BS - CUT % BS), :]
        return carry

    lax.fori_loop(0, CHUNKS, join, 0)

    def no_block(i, carry):
        bslot[i] = 0
        return carry

    lax.fori_loop(0, KMAX * CS, no_block, 0, unroll=8)
    to_scalar.wait()

    def place(i, carry):
        for s in range(SB):
            k = sinfo[CHUNKS + i, s]
            j = sinfo[CHUNKS + i, SB + s]

            @pl.when(j < CS)
            def _():
                bslot[k * CS + j] = (1 << 29) + (i * (BR // 16) + (INFO + s * BS) // 16) * 4 + j

        return carry

    lax.fori_loop(0, PARTS, place, 0)

    def listed(i, carry):
        n, n_mid = carry
        c = tab[0, i]
        low = tab[1, i] // 16
        for s in range(SA):
            r = sinfo[i, s]
            k = sinfo[i, SA + s] * CHUNKS + c
            live = (r < RB).astype(jnp.int32)
            if s < CUT // BS:
                row = i * (UR // 16) + (INFO + s * BS) // 16
            elif s == CUT // BS:
                row = i * (BS // 16)
            else:
                row = low + (s * BS - CUT) // 16
            word = row * (1 << 17) + r * (1 << 12)
            for j in range(CS):
                e = bslot[k * CS + j]
                there = (e >> 29) & live
                if s == CUT // BS:
                    work_mid[n_mid] = word + (e & 0xFFF)
                    n_mid = n_mid + there
                else:
                    work[n] = word + (e & 0xFFF)
                    n = n + there
        return n, n_mid

    n, n_mid = lax.fori_loop(0, CHUNKS, listed, (jnp.int32(0), jnp.int32(0)))
    for g in range(GROUP):
        work[n + g] = RB << 12
        work_mid[n_mid + g] = RB << 12

    def products(words, rows, count):
        def step(i, carry):
            results = []
            for g in range(GROUP):
                w = words[i * GROUP + g]
                a = rows[pl.ds(pl.multiple_of((w >> 17) * 16, 16), BS), :]
                b = b_ref[pl.ds(pl.multiple_of(((w >> 2) & 0x3FF) * 16, 16), BS), :]
                results.append(jnp.dot(a, b, preferred_element_type=jnp.float32))
            for g in range(GROUP):
                w = words[i * GROUP + g]
                out[(w >> 12) & 31, :, pl.ds(pl.multiple_of((w & 3) * BS, BS), BS)] += results[g]
            return carry

        lax.fori_loop(0, (count + GROUP - 1) // GROUP, step, 0)

    products(work, a_ref, n)
    products(work_mid, mid, n_mid)
    done = pltpu.make_async_copy(out.at[pl.ds(0, RB)], o_hbm, sem.at[1])
    done.start()
    done.wait()


def multiply(tab, a_all, b_all):
    vmem = pl.BlockSpec(memory_space=pltpu.VMEM)
    return pl.pallas_call(
        kernel,
        out_shape=jax.ShapeDtypeStruct((RB, BS, CS * BS), jnp.float32),
        in_specs=[pl.BlockSpec(memory_space=pltpu.SMEM), vmem, vmem],
        out_specs=pl.BlockSpec(memory_space=pl.ANY),
        scratch_shapes=[
            pltpu.VMEM((RB + 1, BS, CS * BS), jnp.float32),
            pltpu.VMEM((CHUNKS * BS, BS), jnp.bfloat16),
            pltpu.SMEM((KMAX * CS,), jnp.int32),
            pltpu.SMEM((LIST,), jnp.int32),
            pltpu.SMEM((LIST,), jnp.int32),
            pltpu.VMEM((CHUNKS + PARTS, BS), jnp.int32),
            pltpu.SMEM((CHUNKS + PARTS, BS), jnp.int32),
            pltpu.SemaphoreType.DMA((2,)),
        ],
        compiler_params=pltpu.CompilerParams(vmem_limit_bytes=40 * 2**20),
        cost_estimate=pl.CostEstimate(flops=10**9, bytes_accessed=13 * 10**6, transcendentals=0),
    )(tab, a_all, b_all)


def body(a_blocks, a_where, b_blocks, b_where):
    rows = a_blocks.reshape(SA * BS, BS)
    u = with_info(a_where[:, 0], a_where[:, 1] // CHUNKS, rows[:CUT])
    v = rows[CUT:]
    b = with_info(b_where[:, 0], b_where[:, 1], b_blocks.reshape(SB * BS, BS))

    u1, um1 = along_z(u, -1), along_z(u, 1)
    v1, vm1 = along_x(v, -1), along_x(v, 1)
    u2, um2 = along_z(u1, -1), along_z(um1, 1)
    v2 = along_x(v1, -1)
    u3, um3 = along_z(u2, -1), along_z(um2, 1)
    w = cat([v, v1, vm1, v2])
    w, u3, um3 = tie(w, u3, um3)
    u4 = along_z(u3, -1)
    w1, wm1 = along_z(w, -1), along_z(w, 1)
    x = cat([u, u1, um1, u2, um2, u3, um3, u4])
    x, b = tie(x, b)
    xp, xm = along_x(x, -1), along_x(x, 1)
    by1 = along_y(b, -1)
    w1, wm1, by1, b = tie(w1, wm1, by1, b)
    w2, wm2 = along_z(w1, -1), along_z(wm1, 1)
    bm1 = along_y(b, 1)
    w2, wm2, xp, xm, bm1, by1 = tie(w2, wm2, xp, xm, bm1, by1)
    half = NZ // 2 * UR
    xh0, xh1 = along_x(xp[:half], -1), along_x(xm[half:], 1)
    w3, wm3 = along_z(w2, -1), along_z(wm2, 1)
    by2 = along_y(by1, -1)
    w3, wm3, by2 = tie(w3, wm3, by2)
    mine = cat([b, by1, bm1, by2])
    other = other_core(mine)
    half = NX // 2 * VR
    wh0, wh1 = along_z(w3[:half], -1), along_z(wm3[half:], 1)

    a_all = cat([x, xp, xm, xh0, xh1, w, w1, wm1, w2, wm2, w3, wm3, wh0, wh1])
    b_all = cat([mine, other])

    u_order, v_order = np.array(U_ORDER), np.array(V_ORDER)
    place = {(dz % NZ, dx % NX): i for i, (dz, dx) in enumerate(V_ORDER)}
    v_row = [CHUNKS * UR + place[dz % NZ, dx % NX] * VR for dz, dx in U_ORDER]
    chunk = (lax.axis_index("col") + u_order[:, 0]) % NZ * NX + (lax.axis_index("layer") + u_order[:, 1]) % NX
    tab = jnp.stack([chunk.astype(jnp.int32), jnp.array(v_row, jnp.int32)])
    return multiply(tab, a_all, b_all).reshape(RB * BS, CS * BS)


def solution(mesh):
    in_specs = (
        P(("row", "col", "layer"), None, None),
        P(("row", "col", "layer"), None),
        P(("row", "col", "layer"), None, None),
        P(("row", "col", "layer"), None),
    )
    out_specs = P("row", ("col", "layer"))
    return jax.shard_map(body, mesh=mesh, in_specs=in_specs, out_specs=out_specs, check_vma=False)
```

time: 311 us -> 94.1 us (0.30)
  other arithmetic: 105 us -> 4.63 us
  blocking collectives: 53.6 us -> 0 us
  local copies, waits for them, and re-layouts: 46.9 us -> 3.12 us
  matrix products: 43.7 us -> 0 us
  starting transfers between devices: 0.04 us -> 34.8 us
  between operations: 13.4 us -> 0.5 us
  Pallas kernels: 0 us -> 9.25 us
  waiting for transfers between devices: 46.2 us -> 41.7 us
    scatter-add x3 -> x0, other arithmetic: 104 us -> none  [one_group(): return (acc.at[group_where[:, 0]].add(partial_rows, mode='drop'), None)]
    all_gather x2 -> x0, blocking collectives: 53.6 us -> none  [the longest x1 44.8 us: body(): lax.all_gather(a_where, ('col', 'layer'), axis=0, tiled=True)]
    all_gather x2 -> x0, waiting for transfers between devices: 44.8 us -> none  [the longest x1 44.8 us: body(): lax.all_gather(a_blocks, ('col', 'layer'), axis=0, tiled=True)]
    dot_general x4 -> x0, matrix products: 43.7 us -> none  [the longest x3 36.5 us: one_group(): jnp.einsum('gab,gbc->gac', group_blocks, strips, preferred_element_type=j...]
    ppermute x0 -> x26, waiting for transfers between devices: none -> 41.7 us  [the longest x15 22.5 us: along_z(): return lax.ppermute(x, 'col', [(i, (i + d) % NZ) for i in range(NZ)])]
    ppermute x0 -> x26, starting transfers between devices: none -> 34.8 us  [the longest x15 22.9 us: along_z(): return lax.ppermute(x, 'col', [(i, (i + d) % NZ) for i in range(NZ)])]
    gather x3 -> x0, local copies, waits for them, and re-layouts: 26.7 us -> none  [one_group(): strips = jnp.take(dense, group_where[:, 1], axis=0)]
    pallas_call x0 -> x1, Pallas kernels: none -> 9.25 us  [multiply(): pl.pallas_call(kernel, out_shape=jax.ShapeDtypeStruct((RB, BS, CS * BS),...]
  transfers between devices with their start and end apart: 2 -> 26, of which waited for: 1 -> 14; matrix products, arithmetic and copies ran while one was open for 8% -> 5% of each run, Pallas kernels for 0% -> 0%
where the time goes in v1:
time: 94.1 us; the launch traced here: 94 us
  waiting for transfers between devices  41.7 us (44%)
  starting transfers between devices  34.8 us (37%)
  Pallas kernels  9.25 us (10%)
  other arithmetic  4.63 us (5%)
  local copies, waits for them, and re-layouts  3.12 us (3%)
    ppermute x15, starting transfers between devices, along_z(): return lax.ppermute(x, 'col', [(i, (i + d) % NZ) for i in range(NZ)])  22.9 us
    ppermute x15, waiting for transfers between devices, along_z(): return lax.ppermute(x, 'col', [(i, (i + d) % NZ) for i in range(NZ)])  22.5 us
    ppermute x3, waiting for transfers between devices, along_y(): return lax.ppermute(x, 'row', [(i, (i + 2 * d) % n) for i in range(n)])  18.9 us
    ppermute x7, starting transfers between devices, along_x(): return lax.ppermute(x, 'layer', [(i, (i + d) % NX) for i in range(NX)])  10.6 us
    pallas_call x1, Pallas kernels, multiply(): pl.pallas_call(kernel, out_shape=jax.ShapeDtypeStruct((RB, BS, CS * BS),...  9.25 us
  transfers between devices with their start and end apart: 26, of which 14 were waited for; matrix products, arithmetic and copies ran while one was open for 5% of the time, Pallas kernels for 0%

profile of v1, /device:TPU:24, one launch (start us, length us, event | category | flops | bytes accessed | tf_op | source)
XLA Modules:
  0.0 94.0 jit_solution(16830088700436255294)
XLA Ops:
  2.4 5.9 %collective-permute-start = (bf16[464,128]{1,0:T(8,128)(2,1)S(1)}, bf16[464,128]{1,0:T(8,128)(2,1)S(1)}, u32[]{:S(2)}, u32[]{:S(2)}) collective-permute-start(bf16[464,128]{1,0:T(8,128)(2,1)S(1)} %pad_maximum_fusion.3), channel_id=1, source_target_pairs={{0,28},{4,0},{8,4},{12,8},{16,12},{20,16},{24,20},{28,24},{1,29},{... | collective-permute-start | bytes 356360 | tf_op jit(solution)/shard_map/ppermute | solution.py:43
  9.2 2.8 %collective-permute-start.4 = (bf16[320,128]{1,0:T(8,128)(2,1)S(1)}, bf16[320,128]{1,0:T(8,128)(2,1)S(1)}, u32[]{:S(2)}, u32[]{:S(2)}) collective-permute-start(bf16[320,128]{1,0:T(8,128)(2,1)S(1)} %slice.76), channel_id=1, source_target_pairs={{0,3},{1,0},{2,1},{3,2},{4,7},{5,4},{6,5},{7,6},{8,11},{9,8},{10,9... | collective-permute-start | bytes 245768 | tf_op jit(solution)/shard_map/ppermute | solution.py:47
  12.8 1.0 %pad_maximum_fusion.2 = bf16[1040,128]{1,0:T(8,128)(2,1)S(1)} fusion(bf16[1024,128]{1,0:T(8,128)(2,1)} %bitcast.23, bf16[16,128]{1,0:T(8,128)(2,1)S(1)} %fusion.10), kind=kLoop, calls=%fused_computation.2 | loop fusion | flops 532480 | bytes 532480 | tf_op jit(solution)/shard_map/concatenate | solution.py:35
  14.1 3.6 %collective-permute-start.6 = (bf16[320,128]{1,0:T(8,128)(2,1)S(1)}, bf16[320,128]{1,0:T(8,128)(2,1)S(1)}, u32[]{:S(2)}, u32[]{:S(2)}) collective-permute-start(bf16[320,128]{1,0:T(8,128)(2,1)S(1)} %collective-permute-done.4), channel_id=1, source_target_pairs={{0,3},{1,0},{2,1},{3,2},{4,7},{5,4},{6,5},{7,6},{8,11},{9,8},{10,9... | collective-permute-start | bytes 245768 | tf_op jit(solution)/shard_map/ppermute | solution.py:47
  17.7 3.2 %collective-permute-start.2 = (bf16[464,128]{1,0:T(8,128)(2,1)S(1)}, bf16[464,128]{1,0:T(8,128)(2,1)S(1)}, u32[]{:S(2)}, u32[]{:S(2)}) collective-permute-start(bf16[464,128]{1,0:T(8,128)(2,1)S(1)} %collective-permute-done), channel_id=1, source_target_pairs={{0,28},{4,0},{8,4},{12,8},{16,12},{20,16},{24,20},{28,24},{1,29},{... | collective-permute-start | bytes 356360 | tf_op jit(solution)/shard_map/ppermute | solution.py:43
  21.1 2.2 %collective-permute-done.2 = bf16[464,128]{1,0:T(8,128)(2,1)S(1)} collective-permute-done((bf16[464,128]{1,0:T(8,128)(2,1)S(1)}, bf16[464,128]{1,0:T(8,128)(2,1)S(1)}, u32[]{:S(2)}, u32[]{:S(2)}) %collective-permute-start.2) | collective-permute-done | bytes 118816 | tf_op jit(solution)/shard_map/ppermute | solution.py:43
  23.3 3.6 %collective-permute-start.7 = (bf16[464,128]{1,0:T(8,128)(2,1)S(1)}, bf16[464,128]{1,0:T(8,128)(2,1)S(1)}, u32[]{:S(2)}, u32[]{:S(2)}) collective-permute-start(bf16[464,128]{1,0:T(8,128)(2,1)S(1)} %collective-permute-done.2), channel_id=1, source_target_pairs={{0,28},{4,0},{8,4},{12,8},{16,12},{20,16},{24,20},{28,24},{1,29},{... | collective-permute-start | bytes 356360 | tf_op jit(solution)/shard_map/ppermute | solution.py:43
  27.1 2.8 %collective-permute-done.7 = bf16[464,128]{1,0:T(8,128)(2,1)S(1)} collective-permute-done((bf16[464,128]{1,0:T(8,128)(2,1)S(1)}, bf16[464,128]{1,0:T(8,128)(2,1)S(1)}, u32[]{:S(2)}, u32[]{:S(2)}) %collective-permute-start.7) | collective-permute-done | bytes 118816 | tf_op jit(solution)/shard_map/ppermute | solution.py:43
  29.9 4.2 %collective-permute-done.8 = bf16[464,128]{1,0:T(8,128)(2,1)S(1)} collective-permute-done((bf16[464,128]{1,0:T(8,128)(2,1)S(1)}, bf16[464,128]{1,0:T(8,128)(2,1)S(1)}, u32[]{:S(2)}, u32[]{:S(2)}) %collective-permute-start.8) | collective-permute-done | bytes 118816 | tf_op jit(solution)/shard_map/ppermute | solution.py:43
  34.1 2.0 %collective-permute-start.11 = (bf16[1280,128]{1,0:T(8,128)(2,1)S(1)}, bf16[1280,128]{1,0:T(8,128)(2,1)S(1)}, u32[]{:S(2)}, u32[]{:S(2)}) collective-permute-start(bf16[1280,128]{1,0:T(8,128)(2,1)S(1)} %pad_maximum_fusion.1), channel_id=1, source_target_pairs={{0,4},{4,8},{8,12},{12,16},{16,20},{20,24},{24,28},{28,0},{1,5},{5... | collective-permute-start | bytes 983048 | tf_op jit(solution)/shard_map/ppermute | solution.py:43
  36.1 1.2 %collective-permute-start.9 = (bf16[464,128]{1,0:T(8,128)(2,1)S(1)}, bf16[464,128]{1,0:T(8,128)(2,1)S(1)}, u32[]{:S(2)}, u32[]{:S(2)}) collective-permute-start(bf16[464,128]{1,0:T(8,128)(2,1)S(1)} %collective-permute-done.7), channel_id=1, source_target_pairs={{0,28},{4,0},{8,4},{12,8},{16,12},{20,16},{24,20},{28,24},{1,29},{... | collective-permute-start | bytes 356360 | tf_op jit(solution)/shard_map/ppermute | solution.py:43
  37.4 5.1 %collective-permute-done.9 = bf16[464,128]{1,0:T(8,128)(2,1)S(1)} collective-permute-done((bf16[464,128]{1,0:T(8,128)(2,1)S(1)}, bf16[464,128]{1,0:T(8,128)(2,1)S(1)}, u32[]{:S(2)}, u32[]{:S(2)}) %collective-permute-start.9) | collective-permute-done | bytes 118816 | tf_op jit(solution)/shard_map/ppermute | solution.py:43
  42.6 2.0 %collective-permute-start.16 = (bf16[3712,128]{1,0:T(8,128)(2,1)S(1)}, bf16[3712,128]{1,0:T(8,128)(2,1)S(1)}, u32[]{:S(2)}, u32[]{:S(2)}) collective-permute-start(bf16[3712,128]{1,0:T(8,128)(2,1)S(1)} %constant_dynamic-update-slice_fusion), channel_id=1, source_target_pairs={{0,1},{1,2},{2,3},{3,0},{4,5},{5,6},{6,7},{7,4},{8,9},{9,10},{10,1... | collective-permute-start | bytes 2850824 | tf_op jit(solution)/shard_map/ppermute | solution.py:47
  46.7 5.5 %collective-permute-done.12 = bf16[1040,128]{1,0:T(8,128)(2,1)S(1)} collective-permute-done((bf16[1040,128]{1,0:T(8,128)(2,1)S(1)}, bf16[1040,128]{1,0:T(8,128)(2,1)S(1)}, u32[]{:S(2)}, u32[]{:S(2)}) %collective-permute-start.12) | collective-permute-done | bytes 266272 | tf_op jit(solution)/shard_map/ppermute | solution.py:52
  52.2 1.2 %collective-permute-start.13 = (bf16[1280,128]{1,0:T(8,128)(2,1)S(1)}, bf16[1280,128]{1,0:T(8,128)(2,1)S(1)}, u32[]{:S(2)}, u32[]{:S(2)}) collective-permute-start(bf16[1280,128]{1,0:T(8,128)(2,1)S(1)} %collective-permute-done.10), channel_id=1, source_target_pairs={{0,28},{4,0},{8,4},{12,8},{16,12},{20,16},{24,20},{28,24},{1,29},{... | collective-permute-start | bytes 983048 | tf_op jit(solution)/shard_map/ppermute | solution.py:43
  54.3 6.3 %collective-permute-done.17 = bf16[1040,128]{1,0:T(8,128)(2,1)S(1)} collective-permute-done((bf16[1040,128]{1,0:T(8,128)(2,1)S(1)}, bf16[1040,128]{1,0:T(8,128)(2,1)S(1)}, u32[]{:S(2)}, u32[]{:S(2)}) %collective-permute-start.17) | collective-permute-done | bytes 266272 | tf_op jit(solution)/shard_map/ppermute | solution.py:52
  61.2 1.8 %collective-permute-done.14 = bf16[1280,128]{1,0:T(8,128)(2,1)S(1)} collective-permute-done((bf16[1280,128]{1,0:T(8,128)(2,1)S(1)}, bf16[1280,128]{1,0:T(8,128)(2,1)S(1)}, u32[]{:S(2)}, u32[]{:S(2)}) %collective-permute-start.14) | collective-permute-done | bytes 327712 | tf_op jit(solution)/shard_map/ppermute | solution.py:43
  64.3 1.2 %collective-permute-start.19 = (bf16[1856,128]{1,0:T(8,128)(2,1)S(1)}, bf16[1856,128]{1,0:T(8,128)(2,1)S(1)}, u32[]{:S(2)}, u32[]{:S(2)}) collective-permute-start(bf16[1856,128]{1,0:T(8,128)(2,1)S(1)} %slice.72), channel_id=1, source_target_pairs={{0,1},{1,2},{2,3},{3,0},{4,5},{5,6},{6,7},{7,4},{8,9},{9,10},{10,1... | collective-permute-start | bytes 1425416 | tf_op jit(solution)/shard_map/ppermute | solution.py:47
  65.4 1.4 %collective-permute-start.20 = (bf16[1280,128]{1,0:T(8,128)(2,1)S(1)}, bf16[1280,128]{1,0:T(8,128)(2,1)S(1)}, u32[]{:S(2)}, u32[]{:S(2)}) collective-permute-start(bf16[1280,128]{1,0:T(8,128)(2,1)S(1)} %collective-permute-done.13), channel_id=1, source_target_pairs={{0,28},{4,0},{8,4},{12,8},{16,12},{20,16},{24,20},{28,24},{1,29},{... | collective-permute-start | bytes 983048 | tf_op jit(solution)/shard_map/ppermute | solution.py:43
  68.0 7.1 %collective-permute-done.22 = bf16[1040,128]{1,0:T(8,128)(2,1)S(1)} collective-permute-done((bf16[1040,128]{1,0:T(8,128)(2,1)S(1)}, bf16[1040,128]{1,0:T(8,128)(2,1)S(1)}, u32[]{:S(2)}, u32[]{:S(2)}) %collective-permute-start.22) | collective-permute-done | bytes 266272 | tf_op jit(solution)/shard_map/ppermute | solution.py:52
  75.1 2.7 %collective-permute-start.23 = (bf16[640,128]{1,0:T(8,128)(2,1)S(1)}, bf16[640,128]{1,0:T(8,128)(2,1)S(1)}, u32[]{:S(2)}, u32[]{:S(2)}) collective-permute-start(bf16[640,128]{1,0:T(8,128)(2,1)S(1)} %slice.73), channel_id=1, source_target_pairs={{0,28},{4,0},{8,4},{12,8},{16,12},{20,16},{24,20},{28,24},{1,29},{... | collective-permute-start | bytes 491528 | tf_op jit(solution)/shard_map/ppermute | solution.py:43
  78.7 2.0 %collective-permute-done.23 = bf16[640,128]{1,0:T(8,128)(2,1)S(1)} collective-permute-done((bf16[640,128]{1,0:T(8,128)(2,1)S(1)}, bf16[640,128]{1,0:T(8,128)(2,1)S(1)}, u32[]{:S(2)}, u32[]{:S(2)}) %collective-permute-start.23) | collective-permute-done | bytes 163872 | tf_op jit(solution)/shard_map/ppermute | solution.py:43
  80.7 3.8 %collective-permute-done.24 = bf16[640,128]{1,0:T(8,128)(2,1)S(1)} collective-permute-done((bf16[640,128]{1,0:T(8,128)(2,1)S(1)}, bf16[640,128]{1,0:T(8,128)(2,1)S(1)}, u32[]{:S(2)}, u32[]{:S(2)}) %collective-permute-start.24) | collective-permute-done | bytes 163872 | tf_op jit(solution)/shard_map/ppermute | solution.py:43
  84.6 9.2 %shard_map.73 = f32[16,128,512]{2,1,0:T(8,128)} custom-call(s32[2,32]{1,0:T(2,128)S(1)} %pad_add_fusion.tab, bf16[25088,128]{1,0:T(8,128)(2,1)S(1)} %constant_dynamic-update-slice_fusion.9.a_ref, bf16[8320,128]{1,0:T(8,128)(2,1)S(1)} %constant_dynamic-update-slice_fusion.23.b_ref), custom_call_target="tpu_custom_call" | custom-call | flops 1000000000 | bytes 13000000 | tf_op jit(solution)/shard_map/pallas_call | solution.py:166
  (74 shorter events, 11.8 us)
Async XLA Ops:
  2.4 15.2 %collective-permute-start = (bf16[464,128]{1,0:T(8,128)(2,1)S(1)}, bf16[464,128]{1,0:T(8,128)(2,1)S(1)}, u32[]{:S(2)}, u32[]{:S(2)}) collective-permute-start(bf16[464,128]{1,0:T(8,128)(2,1)S(1)} %pad_maximum_fusion.3), channel_id=1, source_target_pairs={{0,28},{4,0},{8,4},{12,8},{16,12},{20,16},{24,20},{28,24},{1,29},{... | collective-permute-start | bytes 356360 | tf_op jit(solution)/shard_map/ppermute | solution.py:43
  8.3 12.6 %collective-permute-start.1 = (bf16[464,128]{1,0:T(8,128)(2,1)S(1)}, bf16[464,128]{1,0:T(8,128)(2,1)S(1)}, u32[]{:S(2)}, u32[]{:S(2)}) collective-permute-start(bf16[464,128]{1,0:T(8,128)(2,1)S(1)} %pad_maximum_fusion.3), channel_id=1, source_target_pairs={{0,4},{4,8},{8,12},{12,16},{16,20},{20,24},{24,28},{28,0},{1,5},{5... | collective-permute-start | bytes 356360 | tf_op jit(solution)/shard_map/ppermute | solution.py:43
  12.0 9.0 %collective-permute-start.5 = (bf16[320,128]{1,0:T(8,128)(2,1)S(1)}, bf16[320,128]{1,0:T(8,128)(2,1)S(1)}, u32[]{:S(2)}, u32[]{:S(2)}) collective-permute-start(bf16[320,128]{1,0:T(8,128)(2,1)S(1)} %slice.76), channel_id=1, source_target_pairs={{0,1},{1,2},{2,3},{3,0},{4,5},{5,6},{6,7},{7,4},{8,9},{9,10},{10,1... | collective-permute-start | bytes 245768 | tf_op jit(solution)/shard_map/ppermute | solution.py:47
  14.1 7.0 %collective-permute-start.6 = (bf16[320,128]{1,0:T(8,128)(2,1)S(1)}, bf16[320,128]{1,0:T(8,128)(2,1)S(1)}, u32[]{:S(2)}, u32[]{:S(2)}) collective-permute-start(bf16[320,128]{1,0:T(8,128)(2,1)S(1)} %collective-permute-done.4), channel_id=1, source_target_pairs={{0,3},{1,0},{2,1},{3,2},{4,7},{5,4},{6,5},{7,6},{8,11},{9,8},{10,9... | collective-permute-start | bytes 245768 | tf_op jit(solution)/shard_map/ppermute | solution.py:47
  17.7 5.6 %collective-permute-start.2 = (bf16[464,128]{1,0:T(8,128)(2,1)S(1)}, bf16[464,128]{1,0:T(8,128)(2,1)S(1)}, u32[]{:S(2)}, u32[]{:S(2)}) collective-permute-start(bf16[464,128]{1,0:T(8,128)(2,1)S(1)} %collective-permute-done), channel_id=1, source_target_pairs={{0,28},{4,0},{8,4},{12,8},{16,12},{20,16},{24,20},{28,24},{1,29},{... | collective-permute-start | bytes 356360 | tf_op jit(solution)/shard_map/ppermute | solution.py:43
  20.9 6.1 %collective-permute-start.3 = (bf16[464,128]{1,0:T(8,128)(2,1)S(1)}, bf16[464,128]{1,0:T(8,128)(2,1)S(1)}, u32[]{:S(2)}, u32[]{:S(2)}) collective-permute-start(bf16[464,128]{1,0:T(8,128)(2,1)S(1)} %collective-permute-done.1), channel_id=1, source_target_pairs={{0,4},{4,8},{8,12},{12,16},{16,20},{20,24},{24,28},{28,0},{1,5},{5... | collective-permute-start | bytes 356360 | tf_op jit(solution)/shard_map/ppermute | solution.py:43
  23.3 6.6 %collective-permute-start.7 = (bf16[464,128]{1,0:T(8,128)(2,1)S(1)}, bf16[464,128]{1,0:T(8,128)(2,1)S(1)}, u32[]{:S(2)}, u32[]{:S(2)}) collective-permute-start(bf16[464,128]{1,0:T(8,128)(2,1)S(1)} %collective-permute-done.2), channel_id=1, source_target_pairs={{0,28},{4,0},{8,4},{12,8},{16,12},{20,16},{24,20},{28,24},{1,29},{... | collective-permute-start | bytes 356360 | tf_op jit(solution)/shard_map/ppermute | solution.py:43
  27.0 7.1 %collective-permute-start.8 = (bf16[464,128]{1,0:T(8,128)(2,1)S(1)}, bf16[464,128]{1,0:T(8,128)(2,1)S(1)}, u32[]{:S(2)}, u32[]{:S(2)}) collective-permute-start(bf16[464,128]{1,0:T(8,128)(2,1)S(1)} %collective-permute-done.3), channel_id=1, source_target_pairs={{0,4},{4,8},{8,12},{12,16},{16,20},{20,24},{24,28},{28,0},{1,5},{5... | collective-permute-start | bytes 356360 | tf_op jit(solution)/shard_map/ppermute | solution.py:43
  34.1 12.6 %collective-permute-start.10 = (bf16[1280,128]{1,0:T(8,128)(2,1)S(1)}, bf16[1280,128]{1,0:T(8,128)(2,1)S(1)}, u32[]{:S(2)}, u32[]{:S(2)}) collective-permute-start(bf16[1280,128]{1,0:T(8,128)(2,1)S(1)} %pad_maximum_fusion.1), channel_id=1, source_target_pairs={{0,28},{4,0},{8,4},{12,8},{16,12},{20,16},{24,20},{28,24},{1,29},{... | collective-permute-start | bytes 983048 | tf_op jit(solution)/shard_map/ppermute | solution.py:43
  34.1 12.6 %collective-permute-start.11 = (bf16[1280,128]{1,0:T(8,128)(2,1)S(1)}, bf16[1280,128]{1,0:T(8,128)(2,1)S(1)}, u32[]{:S(2)}, u32[]{:S(2)}) collective-permute-start(bf16[1280,128]{1,0:T(8,128)(2,1)S(1)} %pad_maximum_fusion.1), channel_id=1, source_target_pairs={{0,4},{4,8},{8,12},{12,16},{16,20},{20,24},{24,28},{28,0},{1,5},{5... | collective-permute-start | bytes 983048 | tf_op jit(solution)/shard_map/ppermute | solution.py:43
  36.1 6.3 %collective-permute-start.9 = (bf16[464,128]{1,0:T(8,128)(2,1)S(1)}, bf16[464,128]{1,0:T(8,128)(2,1)S(1)}, u32[]{:S(2)}, u32[]{:S(2)}) collective-permute-start(bf16[464,128]{1,0:T(8,128)(2,1)S(1)} %collective-permute-done.7), channel_id=1, source_target_pairs={{0,28},{4,0},{8,4},{12,8},{16,12},{20,16},{24,20},{28,24},{1,29},{... | collective-permute-start | bytes 356360 | tf_op jit(solution)/shard_map/ppermute | solution.py:43
  42.5 20.5 %collective-permute-start.15 = (bf16[3712,128]{1,0:T(8,128)(2,1)S(1)}, bf16[3712,128]{1,0:T(8,128)(2,1)S(1)}, u32[]{:S(2)}, u32[]{:S(2)}) collective-permute-start(bf16[3712,128]{1,0:T(8,128)(2,1)S(1)} %constant_dynamic-update-slice_fusion), channel_id=1, source_target_pairs={{0,3},{1,0},{2,1},{3,2},{4,7},{5,4},{6,5},{7,6},{8,11},{9,8},{10,9... | collective-permute-start | bytes 2850824 | tf_op jit(solution)/shard_map/ppermute | solution.py:47
  42.6 20.4 %collective-permute-start.16 = (bf16[3712,128]{1,0:T(8,128)(2,1)S(1)}, bf16[3712,128]{1,0:T(8,128)(2,1)S(1)}, u32[]{:S(2)}, u32[]{:S(2)}) collective-permute-start(bf16[3712,128]{1,0:T(8,128)(2,1)S(1)} %constant_dynamic-update-slice_fusion), channel_id=1, source_target_pairs={{0,1},{1,2},{2,3},{3,0},{4,5},{5,6},{6,7},{7,4},{8,9},{9,10},{10,1... | collective-permute-start | bytes 2850824 | tf_op jit(solution)/shard_map/ppermute | solution.py:47
  44.6 7.6 %collective-permute-start.12 = (bf16[1040,128]{1,0:T(8,128)(2,1)S(1)}, bf16[1040,128]{1,0:T(8,128)(2,1)S(1)}, u32[]{:S(2)}, u32[]{:S(2)}) collective-permute-start(bf16[1040,128]{1,0:T(8,128)(2,1)S(1)} %pad_maximum_fusion.2), channel_id=1, source_target_pairs={{0,192},{32,224},{64,0},{96,32},{128,64},{160,96},{192,128},{224,1... | collective-permute-start | bytes 798728 | tf_op jit(solution)/shard_map/ppermute | solution.py:52
  52.2 9.0 %collective-permute-start.13 = (bf16[1280,128]{1,0:T(8,128)(2,1)S(1)}, bf16[1280,128]{1,0:T(8,128)(2,1)S(1)}, u32[]{:S(2)}, u32[]{:S(2)}) collective-permute-start(bf16[1280,128]{1,0:T(8,128)(2,1)S(1)} %collective-permute-done.10), channel_id=1, source_target_pairs={{0,28},{4,0},{8,4},{12,8},{16,12},{20,16},{24,20},{28,24},{1,29},{... | collective-permute-start | bytes 983048 | tf_op jit(solution)/shard_map/ppermute | solution.py:43
  53.4 9.6 %collective-permute-start.14 = (bf16[1280,128]{1,0:T(8,128)(2,1)S(1)}, bf16[1280,128]{1,0:T(8,128)(2,1)S(1)}, u32[]{:S(2)}, u32[]{:S(2)}) collective-permute-start(bf16[1280,128]{1,0:T(8,128)(2,1)S(1)} %collective-permute-done.11), channel_id=1, source_target_pairs={{0,4},{4,8},{8,12},{12,16},{16,20},{20,24},{24,28},{28,0},{1,5},{5... | collective-permute-start | bytes 983048 | tf_op jit(solution)/shard_map/ppermute | solution.py:43
  54.2 6.4 %collective-permute-start.17 = (bf16[1040,128]{1,0:T(8,128)(2,1)S(1)}, bf16[1040,128]{1,0:T(8,128)(2,1)S(1)}, u32[]{:S(2)}, u32[]{:S(2)}) collective-permute-start(bf16[1040,128]{1,0:T(8,128)(2,1)S(1)} %pad_maximum_fusion.2), channel_id=1, source_target_pairs={{0,64},{32,96},{64,128},{96,160},{128,192},{160,224},{192,0},{224,... | collective-permute-start | bytes 798728 | tf_op jit(solution)/shard_map/ppermute | solution.py:52
  63.3 14.8 %collective-permute-start.18 = (bf16[1856,128]{1,0:T(8,128)(2,1)S(1)}, bf16[1856,128]{1,0:T(8,128)(2,1)S(1)}, u32[]{:S(2)}, u32[]{:S(2)}) collective-permute-start(bf16[1856,128]{1,0:T(8,128)(2,1)S(1)} %slice.71), channel_id=1, source_target_pairs={{0,3},{1,0},{2,1},{3,2},{4,7},{5,4},{6,5},{7,6},{8,11},{9,8},{10,9... | collective-permute-start | bytes 1425416 | tf_op jit(solution)/shard_map/ppermute | solution.py:47
  64.3 14.0 %collective-permute-start.19 = (bf16[1856,128]{1,0:T(8,128)(2,1)S(1)}, bf16[1856,128]{1,0:T(8,128)(2,1)S(1)}, u32[]{:S(2)}, u32[]{:S(2)}) collective-permute-start(bf16[1856,128]{1,0:T(8,128)(2,1)S(1)} %slice.72), channel_id=1, source_target_pairs={{0,1},{1,2},{2,3},{3,0},{4,5},{5,6},{6,7},{7,4},{8,9},{9,10},{10,1... | collective-permute-start | bytes 1425416 | tf_op jit(solution)/shard_map/ppermute | solution.py:47
  65.4 9.7 %collective-permute-start.20 = (bf16[1280,128]{1,0:T(8,128)(2,1)S(1)}, bf16[1280,128]{1,0:T(8,128)(2,1)S(1)}, u32[]{:S(2)}, u32[]{:S(2)}) collective-permute-start(bf16[1280,128]{1,0:T(8,128)(2,1)S(1)} %collective-permute-done.13), channel_id=1, source_target_pairs={{0,28},{4,0},{8,4},{12,8},{16,12},{20,16},{24,20},{28,24},{1,29},{... | collective-permute-start | bytes 983048 | tf_op jit(solution)/shard_map/ppermute | solution.py:43
  66.8 8.3 %collective-permute-start.21 = (bf16[1280,128]{1,0:T(8,128)(2,1)S(1)}, bf16[1280,128]{1,0:T(8,128)(2,1)S(1)}, u32[]{:S(2)}, u32[]{:S(2)}) collective-permute-start(bf16[1280,128]{1,0:T(8,128)(2,1)S(1)} %collective-permute-done.14), channel_id=1, source_target_pairs={{0,4},{4,8},{8,12},{12,16},{16,20},{20,24},{24,28},{28,0},{1,5},{5... | collective-permute-start | bytes 983048 | tf_op jit(solution)/shard_map/ppermute | solution.py:43
  67.4 7.6 %collective-permute-start.22 = (bf16[1040,128]{1,0:T(8,128)(2,1)S(1)}, bf16[1040,128]{1,0:T(8,128)(2,1)S(1)}, u32[]{:S(2)}, u32[]{:S(2)}) collective-permute-start(bf16[1040,128]{1,0:T(8,128)(2,1)S(1)} %collective-permute-done.12), channel_id=1, source_target_pairs={{0,192},{32,224},{64,0},{96,32},{128,64},{160,96},{192,128},{224,1... | collective-permute-start | bytes 798728 | tf_op jit(solution)/shard_map/ppermute | solution.py:52
  77.8 6.6 %collective-permute-start.24 = (bf16[640,128]{1,0:T(8,128)(2,1)S(1)}, bf16[640,128]{1,0:T(8,128)(2,1)S(1)}, u32[]{:S(2)}, u32[]{:S(2)}) collective-permute-start(bf16[640,128]{1,0:T(8,128)(2,1)S(1)} %slice.74), channel_id=1, source_target_pairs={{0,4},{4,8},{8,12},{12,16},{16,20},{20,24},{24,28},{28,0},{1,5},{5... | collective-permute-start | bytes 491528 | tf_op jit(solution)/shard_map/ppermute | solution.py:43
  78.0 6.5 %collective-permute-start.25 = (bf16[4160,128]{1,0:T(8,128)(2,1)S(1)}, bf16[4160,128]{1,0:T(8,128)(2,1)S(1)}, u32[]{:S(2)}, u32[]{:S(2)}) collective-permute-start(bf16[4160,128]{1,0:T(8,128)(2,1)S(1)} %pad_maximum_fusion), channel_id=1, source_target_pairs={{0,32},{32,0},{64,96},{96,64},{128,160},{160,128},{192,224},{224,1... | collective-permute-start | bytes 3194888 | tf_op jit(solution)/shard_map/ppermute | solution.py:56
  (2 other events, 10.3 us)

commit v2 on v0

v2 whole, which is shorter than its diff:
```python
import functools

import jax
import jax.numpy as jnp
from jax import lax
from jax.experimental import pallas as pl
from jax.experimental.pallas import tpu as pltpu
from jax.sharding import PartitionSpec as P

BS = 128
RB = 16
CS = 4
SA = 6
SB = 8
NZ = 8
NX = 4
NY = 4
INFO = 16
CUT = 512
UR = INFO + CUT
VR = SA * BS - CUT
BR = INFO + SB * BS
CHUNKS = NZ * NX
PARTS = NY * 2
GROUP = 16
LIST = CHUNKS * SA * CS + 2 * GROUP

Z_ORDER = (0, 1, -1, 2, -2, 3, -3, 4)
X_ORDER = (0, 1, -1, 2)
U_ORDER = [(dz, dx) for dx in X_ORDER for dz in Z_ORDER]
V_ORDER = [(dz, dx) for dz in Z_ORDER for dx in X_ORDER]


def cat(pieces):
    return jnp.concatenate(pieces, axis=0)


def after(x, *others):
    return lax.optimization_barrier((x, *others))[0]


def along_z(x, d):
    return lax.ppermute(x, "col", [(i, (i + d) % NZ) for i in range(NZ)])


def along_x(x, d):
    return lax.ppermute(x, "layer", [(i, (i + d) % NX) for i in range(NX)])


def along_y(x, d):
    n = 2 * NY
    return lax.ppermute(x, "row", [(i, (i + 2 * d) % n) for i in range(n)])


def other_core(x):
    return lax.ppermute(x, "row", [(i, i ^ 1) for i in range(2 * NY)])


def with_info(where, blocks):
    tile = jnp.pad(where.T.astype(jnp.bfloat16), ((0, INFO - 2), (0, BS - where.shape[0])))
    return cat([tile, blocks])


def kernel(n_a, *refs):
    a_parts, refs = refs[:n_a], refs[n_a:]
    b_parts, refs = refs[:-11], refs[-11:]
    o_hbm, out, a_ref, b_ref, u_at, v_at, live, work, info, sinfo, sem = refs
    loads = []
    for slot, (parts, whole) in enumerate(((b_parts, b_ref), (a_parts, a_ref))):
        row = 0
        for part in parts:
            rows = part.shape[0]
            loads.append(pltpu.make_async_copy(part, whole.at[pl.ds(row, rows)], sem.at[slot]))
            row += rows
    for load in loads:
        load.start()

    q, t = lax.axis_index("col"), lax.axis_index("layer")
    for order, at, step, base in ((U_ORDER, u_at, 1, 0), (V_ORDER, v_at, VR // 16, CHUNKS * UR // 16)):
        for i, (dz, dx) in enumerate(order):
            at[((q + dz) & (NZ - 1)) * NX + ((t + dx) & (NX - 1))] = base + i * step

    def clear(i, carry):
        out[i] = jnp.zeros((BS, CS * BS), jnp.float32)
        return carry

    lax.fori_loop(0, RB + 1, clear, 0)
    for load in loads:
        load.wait()

    starts = [(a_ref, i * UR) for i in range(CHUNKS)] + [(b_ref, i * BR) for i in range(PARTS)]
    for i, (ref, at) in enumerate(starts):
        tile = ref[at : at + INFO, :].astype(jnp.float32)
        info[i : i + 1, :] = (tile[0:1] * 64 + tile[1:2]).astype(jnp.int32)
    to_scalar = pltpu.make_async_copy(info, sinfo, sem.at[2])
    to_scalar.start()
    to_scalar.wait()

    def found(i, n):
        for s in range(SB):
            v = sinfo[CHUNKS + i, s]
            live[n] = ((v >> 6) << 12) + (i * (BR // 16) + (INFO + s * BS) // 16) * 4 + (v & 3)
            n = n + jnp.where((v & 63) < CS, 1, 0)
        return n

    def listed(i, n):
        b = live[i]
        k, b = b >> 12, b & 0xFFF
        piece, low = u_at[k & (CHUNKS - 1)], v_at[k & (CHUNKS - 1)]
        top = ((piece * (UR // 16) + INFO // 16) << 17) + b
        low = (low << 17) + b
        for s in range(SA):
            x = sinfo[piece, s] ^ k
            work[n] = (top + (s * BS << 13) if s * BS < CUT else low + (s * BS - CUT << 13)) + (x << 6)
            n = n + jnp.where((x & ~((RB - 1) << 6)) == 0, 1, 0)
        return n

    n = lax.fori_loop(0, lax.fori_loop(0, PARTS, found, jnp.int32(0)), listed, jnp.int32(0))
    for g in range(GROUP):
        work[n + g] = RB << 12

    def products(i, carry):
        words = [work[i * GROUP + g] for g in range(GROUP)]
        results = []
        for w in words:
            a = a_ref[pl.ds(pl.multiple_of((w >> 17) * 16, 16), BS), :]
            b = b_ref[pl.ds(pl.multiple_of(((w >> 2) & 0x3FF) * 16, 16), BS), :]
            results.append(jnp.dot(a, b, preferred_element_type=jnp.float32))
        for w, result in zip(words, results):
            out[(w >> 12) & 31, :, pl.ds(pl.multiple_of((w & 3) * BS, BS), BS)] += result
        return carry

    lax.fori_loop(0, (n + GROUP - 1) // GROUP, products, 0)
    stores = [
        pltpu.make_async_copy(out.at[pl.ds(r, 4)], o_hbm.at[pl.ds(r, 4)], sem.at[3]) for r in range(0, RB, 4)
    ]
    for store in stores:
        store.start()
    for store in stores:
        store.wait()


def multiply(a_parts, b_parts):
    hbm = pl.BlockSpec(memory_space=pl.ANY)
    return pl.pallas_call(
        functools.partial(kernel, len(a_parts)),
        out_shape=jax.ShapeDtypeStruct((RB, BS, CS * BS), jnp.float32),
        in_specs=[hbm] * (len(a_parts) + len(b_parts)),
        out_specs=hbm,
        scratch_shapes=[
            pltpu.VMEM((RB + 1, BS, CS * BS), jnp.float32),
            pltpu.VMEM((CHUNKS * (UR + VR), BS), jnp.bfloat16),
            pltpu.VMEM((PARTS * BR, BS), jnp.bfloat16),
            pltpu.SMEM((CHUNKS,), jnp.int32),
            pltpu.SMEM((CHUNKS,), jnp.int32),
            pltpu.SMEM((PARTS * SB + 1,), jnp.int32),
            pltpu.SMEM((LIST,), jnp.int32),
            pltpu.VMEM((CHUNKS + PARTS, BS), jnp.int32),
            pltpu.SMEM((CHUNKS + PARTS, BS), jnp.int32),
            pltpu.SemaphoreType.DMA((4,)),
        ],
        compiler_params=pltpu.CompilerParams(vmem_limit_bytes=20 * 2**20),
        cost_estimate=pl.CostEstimate(flops=10**9, bytes_accessed=13 * 10**6, transcendentals=0),
    )(*a_parts, *b_parts)


def body(a_blocks, a_where, b_blocks, b_where):
    rows = a_blocks.reshape(SA * BS, BS)
    u = with_info(a_where, rows[:CUT])
    b = with_info(b_where, b_blocks.reshape(SB * BS, BS))
    u1, um1 = along_z(u, -1), along_z(u, 1)
    b = cat([b, other_core(b)])
    v = after(rows[CUT:], b)

    v1, vm1 = along_x(v, -1), along_x(v, 1)
    u2, um2 = along_z(u1, -1), along_z(um1, 1)
    by1 = along_y(after(b, u1), -1)
    v2 = along_x(v1, -1)
    u3, um3 = along_z(u2, -1), along_z(um2, 1)
    bm1 = along_y(after(b, u2), 1)
    w = after(cat([v, v1, vm1, v2]), u3, um3)
    u4 = along_z(u3, -1)
    w1, wm1 = along_z(w, -1), along_z(w, 1)
    x = cat([u, u1, um1, u2, um2, u3, um3, u4])
    xp, xm = along_x(x, -1), along_x(x, 1)
    w2, wm2 = along_z(w1, -1), along_z(wm1, 1)
    by2 = along_y(after(by1, w1), -1)
    w3, wm3 = along_z(w2, -1), along_z(wm2, 1)
    half = NZ // 2 * UR
    xh0, xh1 = along_x(after(xp, w3)[:half], -1), along_x(after(xm, wm3)[half:], 1)
    half = NX // 2 * VR
    wh0, wh1 = along_z(w3[:half], -1), along_z(wm3[half:], 1)

    a_parts = [x, xp, xm, xh0, xh1, w, w1, wm1, w2, wm2, w3, wm3, wh0, wh1]
    return multiply(a_parts, [b, by1, bm1, by2]).reshape(RB * BS, CS * BS)


def solution(mesh):
    in_specs = (
        P(("row", "col", "layer"), None, None),
        P(("row", "col", "layer"), None),
        P(("row", "col", "layer"), None, None),
        P(("row", "col", "layer"), None),
    )
    out_specs = P("row", ("col", "layer"))
    return jax.shard_map(body, mesh=mesh, in_specs=in_specs, out_specs=out_specs, check_vma=False)
```

time: 311 us -> 83 us (0.27)
  other arithmetic: 105 us -> 2.44 us
  blocking collectives: 53.6 us -> 0 us
  local copies, waits for them, and re-layouts: 46.9 us -> 2.03 us
  matrix products: 43.7 us -> 0 us
  starting transfers between devices: 0.04 us -> 42.2 us
  waiting for transfers between devices: 46.2 us -> 27.4 us
  between operations: 13.4 us -> 0.35 us
  Pallas kernels: 0 us -> 7.77 us
    scatter-add x3 -> x0, other arithmetic: 104 us -> none  [one_group(): return (acc.at[group_where[:, 0]].add(partial_rows, mode='drop'), None)]
    all_gather x2 -> x0, blocking collectives: 53.6 us -> none  [the longest x1 44.8 us: body(): lax.all_gather(a_where, ('col', 'layer'), axis=0, tiled=True)]
    all_gather x2 -> x0, waiting for transfers between devices: 44.8 us -> none  [the longest x1 44.8 us: body(): lax.all_gather(a_blocks, ('col', 'layer'), axis=0, tiled=True)]
    dot_general x4 -> x0, matrix products: 43.7 us -> none  [the longest x3 36.5 us: one_group(): jnp.einsum('gab,gbc->gac', group_blocks, strips, preferred_element_type=j...]
    ppermute x0 -> x26, starting transfers between devices: none -> 42.2 us  [the longest x15 26.7 us: along_z(): return lax.ppermute(x, 'col', [(i, (i + d) % NZ) for i in range(NZ)])]
    ppermute x0 -> x26, waiting for transfers between devices: none -> 27.4 us  [the longest x15 23.8 us: along_z(): return lax.ppermute(x, 'col', [(i, (i + d) % NZ) for i in range(NZ)])]
    gather x3 -> x0, local copies, waits for them, and re-layouts: 26.7 us -> none  [one_group(): strips = jnp.take(dense, group_where[:, 1], axis=0)]
    unnamed x2 -> x9, local copies, waits for them, and re-layouts: 9.29 us -> 0.14 us
  transfers between devices with their start and end apart: 2 -> 26, of which waited for: 1 -> 9; matrix products, arithmetic and copies ran while one was open for 8% -> 3% of each run, Pallas kernels for 0% -> 0%
where the time goes in v2:
time: 83 us; the launch traced here: 82.2 us
  starting transfers between devices  42.2 us (51%)
  waiting for transfers between devices  27.4 us (33%)
  Pallas kernels  7.77 us (9%)
  other arithmetic  2.44 us (3%)
  local copies, waits for them, and re-layouts  2.03 us (2%)
    ppermute x15, starting transfers between devices, along_z(): return lax.ppermute(x, 'col', [(i, (i + d) % NZ) for i in range(NZ)])  26.7 us
    ppermute x15, waiting for transfers between devices, along_z(): return lax.ppermute(x, 'col', [(i, (i + d) % NZ) for i in range(NZ)])  23.8 us
    ppermute x7, starting transfers between devices, along_x(): return lax.ppermute(x, 'layer', [(i, (i + d) % NX) for i in range(NX)])  12.6 us
    pallas_call x1, Pallas kernels, multiply(): pl.pallas_call(functools.partial(kernel, len(a_parts)), out_shape=jax.Sha...  7.77 us
    ppermute x3, waiting for transfers between devices, along_y(): return lax.ppermute(x, 'row', [(i, (i + 2 * d) % n) for i in range(n)])  3.64 us
    ppermute x3, starting transfers between devices, along_y(): return lax.ppermute(x, 'row', [(i, (i + 2 * d) % n) for i in range(n)])  2.77 us
  transfers between devices with their start and end apart: 26, of which 9 were waited for; matrix products, arithmetic and copies ran while one was open for 3% of the time, Pallas kernels for 0%

profile of v2, /device:TPU:24, one launch (start us, length us, event | category | flops | bytes accessed | tf_op | source)
XLA Modules:
  0.0 82.2 jit_solution(969208549230897298)
XLA Ops:
  1.7 2.0 %collective-permute-start.1 = (bf16[528,128]{1,0:T(8,128)(2,1)S(1)}, bf16[528,128]{1,0:T(8,128)(2,1)S(1)}, u32[]{:S(2)}, u32[]{:S(2)}) collective-permute-start(bf16[528,128]{1,0:T(8,128)(2,1)S(1)} %pad_maximum_fusion.3), channel_id=1, source_target_pairs={{0,4},{4,8},{8,12},{12,16},{16,20},{20,24},{24,28},{28,0},{1,5},{5... | collective-permute-start | bytes 405512 | tf_op jit(solution)/shard_map/ppermute | solution.py:43
  3.7 4.0 %collective-permute-start = (bf16[528,128]{1,0:T(8,128)(2,1)S(1)}, bf16[528,128]{1,0:T(8,128)(2,1)S(1)}, u32[]{:S(2)}, u32[]{:S(2)}) collective-permute-start(bf16[528,128]{1,0:T(8,128)(2,1)S(1)} %pad_maximum_fusion.3), channel_id=1, source_target_pairs={{0,28},{4,0},{8,4},{12,8},{16,12},{20,16},{24,20},{28,24},{1,29},{... | collective-permute-start | bytes 405512 | tf_op jit(solution)/shard_map/ppermute | solution.py:43
  11.2 3.2 %collective-permute-start.2 = (bf16[528,128]{1,0:T(8,128)(2,1)S(1)}, bf16[528,128]{1,0:T(8,128)(2,1)S(1)}, u32[]{:S(2)}, u32[]{:S(2)}) collective-permute-start(bf16[528,128]{1,0:T(8,128)(2,1)S(1)} %collective-permute-done), channel_id=1, source_target_pairs={{0,28},{4,0},{8,4},{12,8},{16,12},{20,16},{24,20},{28,24},{1,29},{... | collective-permute-start | bytes 405512 | tf_op jit(solution)/shard_map/ppermute | solution.py:43
  14.6 1.6 %collective-permute-start.11 = (bf16[256,128]{1,0:T(8,128)(2,1)S(1)}, bf16[256,128]{1,0:T(8,128)(2,1)S(1)}, u32[]{:S(2)}, u32[]{:S(2)}) collective-permute-start(bf16[256,128]{1,0:T(8,128)(2,1)S(1)} %bitcast.12), channel_id=1, source_target_pairs={{0,1},{1,2},{2,3},{3,0},{4,5},{5,6},{6,7},{7,4},{8,9},{9,10},{10,1... | collective-permute-start | bytes 196616 | tf_op jit(solution)/shard_map/ppermute | solution.py:47
  16.1 1.7 %collective-permute-start.10 = (bf16[256,128]{1,0:T(8,128)(2,1)S(1)}, bf16[256,128]{1,0:T(8,128)(2,1)S(1)}, u32[]{:S(2)}, u32[]{:S(2)}) collective-permute-start(bf16[256,128]{1,0:T(8,128)(2,1)S(1)} %bitcast.13), channel_id=1, source_target_pairs={{0,3},{1,0},{2,1},{3,2},{4,7},{5,4},{6,5},{7,6},{8,11},{9,8},{10,9... | collective-permute-start | bytes 196616 | tf_op jit(solution)/shard_map/ppermute | solution.py:47
  17.9 3.2 %collective-permute-start.4 = (bf16[528,128]{1,0:T(8,128)(2,1)S(1)}, bf16[528,128]{1,0:T(8,128)(2,1)S(1)}, u32[]{:S(2)}, u32[]{:S(2)}) collective-permute-start(bf16[528,128]{1,0:T(8,128)(2,1)S(1)} %collective-permute-done.2), channel_id=1, source_target_pairs={{0,28},{4,0},{8,4},{12,8},{16,12},{20,16},{24,20},{28,24},{1,29},{... | collective-permute-start | bytes 405512 | tf_op jit(solution)/shard_map/ppermute | solution.py:43
  21.2 2.6 %collective-permute-start.12 = (bf16[256,128]{1,0:T(8,128)(2,1)S(1)}, bf16[256,128]{1,0:T(8,128)(2,1)S(1)}, u32[]{:S(2)}, u32[]{:S(2)}) collective-permute-start(bf16[256,128]{1,0:T(8,128)(2,1)S(1)} %collective-permute-done.10), channel_id=1, source_target_pairs={{0,3},{1,0},{2,1},{3,2},{4,7},{5,4},{6,5},{7,6},{8,11},{9,8},{10,9... | collective-permute-start | bytes 196616 | tf_op jit(solution)/shard_map/ppermute | solution.py:47
  23.7 3.6 %collective-permute-start.6 = (bf16[528,128]{1,0:T(8,128)(2,1)S(1)}, bf16[528,128]{1,0:T(8,128)(2,1)S(1)}, u32[]{:S(2)}, u32[]{:S(2)}) collective-permute-start(bf16[528,128]{1,0:T(8,128)(2,1)S(1)} %collective-permute-done.4), channel_id=1, source_target_pairs={{0,28},{4,0},{8,4},{12,8},{16,12},{20,16},{24,20},{28,24},{1,29},{... | collective-permute-start | bytes 405512 | tf_op jit(solution)/shard_map/ppermute | solution.py:43
  27.4 2.5 %collective-permute-done.6 = bf16[528,128]{1,0:T(8,128)(2,1)S(1)} collective-permute-done((bf16[528,128]{1,0:T(8,128)(2,1)S(1)}, bf16[528,128]{1,0:T(8,128)(2,1)S(1)}, u32[]{:S(2)}, u32[]{:S(2)}) %collective-permute-start.6) | collective-permute-done | bytes 135200 | tf_op jit(solution)/shard_map/ppermute | solution.py:43
  29.9 1.3 %collective-permute-start.8 = (bf16[4224,128]{1,0:T(8,128)(2,1)S(1)}, bf16[4224,128]{1,0:T(8,128)(2,1)S(1)}, u32[]{:S(2)}, u32[]{:S(2)}) collective-permute-start(bf16[4224,128]{1,0:T(8,128)(2,1)S(1)} %constant_dynamic-update-slice_fusion.refs_0_), channel_id=1, source_target_pairs={{0,1},{1,2},{2,3},{3,0},{4,5},{5,6},{6,7},{7,4},{8,9},{9,10},{10,1... | collective-permute-start | bytes 3244040 | tf_op jit(solution)/shard_map/ppermute | solution.py:47
  31.2 2.0 %collective-permute-start.7 = (bf16[4224,128]{1,0:T(8,128)(2,1)S(1)}, bf16[4224,128]{1,0:T(8,128)(2,1)S(1)}, u32[]{:S(2)}, u32[]{:S(2)}) collective-permute-start(bf16[4224,128]{1,0:T(8,128)(2,1)S(1)} %constant_dynamic-update-slice_fusion.refs_0_), channel_id=1, source_target_pairs={{0,3},{1,0},{2,1},{3,2},{4,7},{5,4},{6,5},{7,6},{8,11},{9,8},{10,9... | collective-permute-start | bytes 3244040 | tf_op jit(solution)/shard_map/ppermute | solution.py:47
  33.4 3.7 %collective-permute-start.13 = (bf16[1024,128]{1,0:T(8,128)(2,1)S(1)}, bf16[1024,128]{1,0:T(8,128)(2,1)S(1)}, u32[]{:S(2)}, u32[]{:S(2)}) collective-permute-start(bf16[1024,128]{1,0:T(8,128)(2,1)S(1)} %pad_maximum_fusion.2.refs_5_), channel_id=1, source_target_pairs={{0,28},{4,0},{8,4},{12,8},{16,12},{20,16},{24,20},{28,24},{1,29},{... | collective-permute-start | bytes 786440 | tf_op jit(solution)/shard_map/ppermute | solution.py:43
  37.1 5.5 %collective-permute-done.17.refs_7_ = bf16[1024,128]{1,0:T(8,128)(2,1)S(1)} collective-permute-done((bf16[1024,128]{1,0:T(8,128)(2,1)S(1)}, bf16[1024,128]{1,0:T(8,128)(2,1)S(1)}, u32[]{:S(2)}, u32[]{:S(2)}) %collective-permute-start.17) | collective-permute-done | bytes 262176 | tf_op jit(solution)/shard_map/ppermute | solution.py:43
  42.6 3.6 %collective-permute-start.14 = (bf16[1024,128]{1,0:T(8,128)(2,1)S(1)}, bf16[1024,128]{1,0:T(8,128)(2,1)S(1)}, u32[]{:S(2)}, u32[]{:S(2)}) collective-permute-start(bf16[1024,128]{1,0:T(8,128)(2,1)S(1)} %collective-permute-done.13.refs_6_), channel_id=1, source_target_pairs={{0,28},{4,0},{8,4},{12,8},{16,12},{20,16},{24,20},{28,24},{1,29},{... | collective-permute-start | bytes 786440 | tf_op jit(solution)/shard_map/ppermute | solution.py:43
  47.0 5.5 %collective-permute-done.18.refs_9_ = bf16[1024,128]{1,0:T(8,128)(2,1)S(1)} collective-permute-done((bf16[1024,128]{1,0:T(8,128)(2,1)S(1)}, bf16[1024,128]{1,0:T(8,128)(2,1)S(1)}, u32[]{:S(2)}, u32[]{:S(2)}) %collective-permute-start.18) | collective-permute-done | bytes 262176 | tf_op jit(solution)/shard_map/ppermute | solution.py:43
  52.4 1.0 %collective-permute-done.14.refs_8_ = bf16[1024,128]{1,0:T(8,128)(2,1)S(1)} collective-permute-done((bf16[1024,128]{1,0:T(8,128)(2,1)S(1)}, bf16[1024,128]{1,0:T(8,128)(2,1)S(1)}, u32[]{:S(2)}, u32[]{:S(2)}) %collective-permute-start.14) | collective-permute-done | bytes 262176 | tf_op jit(solution)/shard_map/ppermute | solution.py:43
  53.5 2.9 %collective-permute-start.15 = (bf16[1024,128]{1,0:T(8,128)(2,1)S(1)}, bf16[1024,128]{1,0:T(8,128)(2,1)S(1)}, u32[]{:S(2)}, u32[]{:S(2)}) collective-permute-start(bf16[1024,128]{1,0:T(8,128)(2,1)S(1)} %collective-permute-done.14.refs_8_), channel_id=1, source_target_pairs={{0,28},{4,0},{8,4},{12,8},{16,12},{20,16},{24,20},{28,24},{1,29},{... | collective-permute-start | bytes 786440 | tf_op jit(solution)/shard_map/ppermute | solution.py:43
  56.3 3.7 %collective-permute-done.19.refs_11_ = bf16[1024,128]{1,0:T(8,128)(2,1)S(1)} collective-permute-done((bf16[1024,128]{1,0:T(8,128)(2,1)S(1)}, bf16[1024,128]{1,0:T(8,128)(2,1)S(1)}, u32[]{:S(2)}, u32[]{:S(2)}) %collective-permute-start.19) | collective-permute-done | bytes 262176 | tf_op jit(solution)/shard_map/ppermute | solution.py:43
  61.1 2.6 %collective-permute-start.16 = (bf16[2112,128]{1,0:T(8,128)(2,1)S(1)}, bf16[2112,128]{1,0:T(8,128)(2,1)S(1)}, u32[]{:S(2)}, u32[]{:S(2)}) collective-permute-start(bf16[2112,128]{1,0:T(8,128)(2,1)S(1)} %slice.28), channel_id=1, source_target_pairs={{0,3},{1,0},{2,1},{3,2},{4,7},{5,4},{6,5},{7,6},{8,11},{9,8},{10,9... | collective-permute-start | bytes 1622024 | tf_op jit(solution)/shard_map/ppermute | solution.py:47
  63.7 1.8 %collective-permute-start.25 = (bf16[2080,128]{1,0:T(8,128)(2,1)S(1)}, bf16[2080,128]{1,0:T(8,128)(2,1)S(1)}, u32[]{:S(2)}, u32[]{:S(2)}) collective-permute-start(bf16[2080,128]{1,0:T(8,128)(2,1)S(1)} %collective-permute-done.23.refs_15_), channel_id=1, source_target_pairs={{0,192},{32,224},{64,0},{96,32},{128,64},{160,96},{192,128},{224,1... | collective-permute-start | bytes 1597448 | tf_op jit(solution)/shard_map/ppermute | solution.py:52
  65.7 3.6 %collective-permute-done.24.refs_16_ = bf16[2080,128]{1,0:T(8,128)(2,1)S(1)} collective-permute-done((bf16[2080,128]{1,0:T(8,128)(2,1)S(1)}, bf16[2080,128]{1,0:T(8,128)(2,1)S(1)}, u32[]{:S(2)}, u32[]{:S(2)}) %collective-permute-start.24) | collective-permute-done | bytes 532512 | tf_op jit(solution)/shard_map/ppermute | solution.py:52
  69.6 2.2 %collective-permute-done.22.refs_13_ = bf16[512,128]{1,0:T(8,128)(2,1)S(1)} collective-permute-done((bf16[512,128]{1,0:T(8,128)(2,1)S(1)}, bf16[512,128]{1,0:T(8,128)(2,1)S(1)}, u32[]{:S(2)}, u32[]{:S(2)}) %collective-permute-start.22) | collective-permute-done | bytes 131104 | tf_op jit(solution)/shard_map/ppermute | solution.py:43
  71.8 2.5 %collective-permute-done.21.refs_12_ = bf16[512,128]{1,0:T(8,128)(2,1)S(1)} collective-permute-done((bf16[512,128]{1,0:T(8,128)(2,1)S(1)}, bf16[512,128]{1,0:T(8,128)(2,1)S(1)}, u32[]{:S(2)}, u32[]{:S(2)}) %collective-permute-start.21) | collective-permute-done | bytes 131104 | tf_op jit(solution)/shard_map/ppermute | solution.py:43
  74.3 7.8 %shard_map.46 = f32[16,128,512]{2,1,0:T(8,128)} custom-call(bf16[4224,128]{1,0:T(8,128)(2,1)S(1)} %constant_dynamic-update-slice_fusion.refs_0_, bf16[4224,128]{1,0:T(8,128)(2,1)S(1)} %collective-permute-done.7.refs_1_, bf16[4224,128]{1,0:T(8,128)(2,1)S(1)} %collective-permute-done.8.refs_2_, bf16[2112,128]{1,0:T(8,128)(2,1)S(1)} %collective-permute-done.16.refs_3_, ...), custom_call_target="tpu_custom_call" | custom-call | flops 1000000000 | bytes 13000000 | tf_op jit(solution)/shard_map/pallas_call | solution.py:145
  (53 shorter events, 7.7 us)
Async XLA Ops:
  1.7 9.5 %collective-permute-start.1 = (bf16[528,128]{1,0:T(8,128)(2,1)S(1)}, bf16[528,128]{1,0:T(8,128)(2,1)S(1)}, u32[]{:S(2)}, u32[]{:S(2)}) collective-permute-start(bf16[528,128]{1,0:T(8,128)(2,1)S(1)} %pad_maximum_fusion.3), channel_id=1, source_target_pairs={{0,4},{4,8},{8,12},{12,16},{16,20},{20,24},{24,28},{28,0},{1,5},{5... | collective-permute-start | bytes 405512 | tf_op jit(solution)/shard_map/ppermute | solution.py:43
  3.7 7.5 %collective-permute-start = (bf16[528,128]{1,0:T(8,128)(2,1)S(1)}, bf16[528,128]{1,0:T(8,128)(2,1)S(1)}, u32[]{:S(2)}, u32[]{:S(2)}) collective-permute-start(bf16[528,128]{1,0:T(8,128)(2,1)S(1)} %pad_maximum_fusion.3), channel_id=1, source_target_pairs={{0,28},{4,0},{8,4},{12,8},{16,12},{20,16},{24,20},{28,24},{1,29},{... | collective-permute-start | bytes 405512 | tf_op jit(solution)/shard_map/ppermute | solution.py:43
  9.4 5.1 %collective-permute-start.9 = (bf16[1040,128]{1,0:T(8,128)(2,1)S(1)}, bf16[1040,128]{1,0:T(8,128)(2,1)S(1)}, u32[]{:S(2)}, u32[]{:S(2)}) collective-permute-start(bf16[1040,128]{1,0:T(8,128)(2,1)S(1)} %pad_maximum_fusion.1), channel_id=1, source_target_pairs={{0,32},{32,0},{64,96},{96,64},{128,160},{160,128},{192,224},{224,1... | collective-permute-start | bytes 798728 | tf_op jit(solution)/shard_map/ppermute | solution.py:56
  11.2 6.7 %collective-permute-start.3 = (bf16[528,128]{1,0:T(8,128)(2,1)S(1)}, bf16[528,128]{1,0:T(8,128)(2,1)S(1)}, u32[]{:S(2)}, u32[]{:S(2)}) collective-permute-start(bf16[528,128]{1,0:T(8,128)(2,1)S(1)} %collective-permute-done.1), channel_id=1, source_target_pairs={{0,4},{4,8},{8,12},{12,16},{16,20},{20,24},{24,28},{28,0},{1,5},{5... | collective-permute-start | bytes 405512 | tf_op jit(solution)/shard_map/ppermute | solution.py:43
  11.2 6.7 %collective-permute-start.2 = (bf16[528,128]{1,0:T(8,128)(2,1)S(1)}, bf16[528,128]{1,0:T(8,128)(2,1)S(1)}, u32[]{:S(2)}, u32[]{:S(2)}) collective-permute-start(bf16[528,128]{1,0:T(8,128)(2,1)S(1)} %collective-permute-done), channel_id=1, source_target_pairs={{0,28},{4,0},{8,4},{12,8},{16,12},{20,16},{24,20},{28,24},{1,29},{... | collective-permute-start | bytes 405512 | tf_op jit(solution)/shard_map/ppermute | solution.py:43
  14.6 18.7 %collective-permute-start.11 = (bf16[256,128]{1,0:T(8,128)(2,1)S(1)}, bf16[256,128]{1,0:T(8,128)(2,1)S(1)}, u32[]{:S(2)}, u32[]{:S(2)}) collective-permute-start(bf16[256,128]{1,0:T(8,128)(2,1)S(1)} %bitcast.12), channel_id=1, source_target_pairs={{0,1},{1,2},{2,3},{3,0},{4,5},{5,6},{6,7},{7,4},{8,9},{9,10},{10,1... | collective-permute-start | bytes 196616 | tf_op jit(solution)/shard_map/ppermute | solution.py:47
  17.9 9.5 %collective-permute-start.5 = (bf16[528,128]{1,0:T(8,128)(2,1)S(1)}, bf16[528,128]{1,0:T(8,128)(2,1)S(1)}, u32[]{:S(2)}, u32[]{:S(2)}) collective-permute-start(bf16[528,128]{1,0:T(8,128)(2,1)S(1)} %collective-permute-done.3), channel_id=1, source_target_pairs={{0,4},{4,8},{8,12},{12,16},{16,20},{20,24},{24,28},{28,0},{1,5},{5... | collective-permute-start | bytes 405512 | tf_op jit(solution)/shard_map/ppermute | solution.py:43
  17.9 5.9 %collective-permute-start.4 = (bf16[528,128]{1,0:T(8,128)(2,1)S(1)}, bf16[528,128]{1,0:T(8,128)(2,1)S(1)}, u32[]{:S(2)}, u32[]{:S(2)}) collective-permute-start(bf16[528,128]{1,0:T(8,128)(2,1)S(1)} %collective-permute-done.2), channel_id=1, source_target_pairs={{0,28},{4,0},{8,4},{12,8},{16,12},{20,16},{24,20},{28,24},{1,29},{... | collective-permute-start | bytes 405512 | tf_op jit(solution)/shard_map/ppermute | solution.py:43
  21.2 12.1 %collective-permute-start.12 = (bf16[256,128]{1,0:T(8,128)(2,1)S(1)}, bf16[256,128]{1,0:T(8,128)(2,1)S(1)}, u32[]{:S(2)}, u32[]{:S(2)}) collective-permute-start(bf16[256,128]{1,0:T(8,128)(2,1)S(1)} %collective-permute-done.10), channel_id=1, source_target_pairs={{0,3},{1,0},{2,1},{3,2},{4,7},{5,4},{6,5},{7,6},{8,11},{9,8},{10,9... | collective-permute-start | bytes 196616 | tf_op jit(solution)/shard_map/ppermute | solution.py:47
  23.7 6.1 %collective-permute-start.6 = (bf16[528,128]{1,0:T(8,128)(2,1)S(1)}, bf16[528,128]{1,0:T(8,128)(2,1)S(1)}, u32[]{:S(2)}, u32[]{:S(2)}) collective-permute-start(bf16[528,128]{1,0:T(8,128)(2,1)S(1)} %collective-permute-done.4), channel_id=1, source_target_pairs={{0,28},{4,0},{8,4},{12,8},{16,12},{20,16},{24,20},{28,24},{1,29},{... | collective-permute-start | bytes 405512 | tf_op jit(solution)/shard_map/ppermute | solution.py:43
  29.9 30.3 %collective-permute-start.8 = (bf16[4224,128]{1,0:T(8,128)(2,1)S(1)}, bf16[4224,128]{1,0:T(8,128)(2,1)S(1)}, u32[]{:S(2)}, u32[]{:S(2)}) collective-permute-start(bf16[4224,128]{1,0:T(8,128)(2,1)S(1)} %constant_dynamic-update-slice_fusion.refs_0_), channel_id=1, source_target_pairs={{0,1},{1,2},{2,3},{3,0},{4,5},{5,6},{6,7},{7,4},{8,9},{9,10},{10,1... | collective-permute-start | bytes 3244040 | tf_op jit(solution)/shard_map/ppermute | solution.py:47
  31.2 29.9 %collective-permute-start.7 = (bf16[4224,128]{1,0:T(8,128)(2,1)S(1)}, bf16[4224,128]{1,0:T(8,128)(2,1)S(1)}, u32[]{:S(2)}, u32[]{:S(2)}) collective-permute-start(bf16[4224,128]{1,0:T(8,128)(2,1)S(1)} %constant_dynamic-update-slice_fusion.refs_0_), channel_id=1, source_target_pairs={{0,3},{1,0},{2,1},{3,2},{4,7},{5,4},{6,5},{7,6},{8,11},{9,8},{10,9... | collective-permute-start | bytes 3244040 | tf_op jit(solution)/shard_map/ppermute | solution.py:47
  33.3 9.3 %collective-permute-start.17 = (bf16[1024,128]{1,0:T(8,128)(2,1)S(1)}, bf16[1024,128]{1,0:T(8,128)(2,1)S(1)}, u32[]{:S(2)}, u32[]{:S(2)}) collective-permute-start(bf16[1024,128]{1,0:T(8,128)(2,1)S(1)} %pad_maximum_fusion.2.refs_5_), channel_id=1, source_target_pairs={{0,4},{4,8},{8,12},{12,16},{16,20},{20,24},{24,28},{28,0},{1,5},{5... | collective-permute-start | bytes 786440 | tf_op jit(solution)/shard_map/ppermute | solution.py:43
  33.4 9.3 %collective-permute-start.13 = (bf16[1024,128]{1,0:T(8,128)(2,1)S(1)}, bf16[1024,128]{1,0:T(8,128)(2,1)S(1)}, u32[]{:S(2)}, u32[]{:S(2)}) collective-permute-start(bf16[1024,128]{1,0:T(8,128)(2,1)S(1)} %pad_maximum_fusion.2.refs_5_), channel_id=1, source_target_pairs={{0,28},{4,0},{8,4},{12,8},{16,12},{20,16},{24,20},{28,24},{1,29},{... | collective-permute-start | bytes 786440 | tf_op jit(solution)/shard_map/ppermute | solution.py:43
  42.6 9.8 %collective-permute-start.18 = (bf16[1024,128]{1,0:T(8,128)(2,1)S(1)}, bf16[1024,128]{1,0:T(8,128)(2,1)S(1)}, u32[]{:S(2)}, u32[]{:S(2)}) collective-permute-start(bf16[1024,128]{1,0:T(8,128)(2,1)S(1)} %collective-permute-done.17.refs_7_), channel_id=1, source_target_pairs={{0,4},{4,8},{8,12},{12,16},{16,20},{20,24},{24,28},{28,0},{1,5},{5... | collective-permute-start | bytes 786440 | tf_op jit(solution)/shard_map/ppermute | solution.py:43
  42.6 10.9 %collective-permute-start.14 = (bf16[1024,128]{1,0:T(8,128)(2,1)S(1)}, bf16[1024,128]{1,0:T(8,128)(2,1)S(1)}, u32[]{:S(2)}, u32[]{:S(2)}) collective-permute-start(bf16[1024,128]{1,0:T(8,128)(2,1)S(1)} %collective-permute-done.13.refs_6_), channel_id=1, source_target_pairs={{0,28},{4,0},{8,4},{12,8},{16,12},{20,16},{24,20},{28,24},{1,29},{... | collective-permute-start | bytes 786440 | tf_op jit(solution)/shard_map/ppermute | solution.py:43
  46.2 17.5 %collective-permute-start.23 = (bf16[2080,128]{1,0:T(8,128)(2,1)S(1)}, bf16[2080,128]{1,0:T(8,128)(2,1)S(1)}, u32[]{:S(2)}, u32[]{:S(2)}) collective-permute-start(bf16[2080,128]{1,0:T(8,128)(2,1)S(1)} %pad_maximum_fusion.refs_14_), channel_id=1, source_target_pairs={{0,192},{32,224},{64,0},{96,32},{128,64},{160,96},{192,128},{224,1... | collective-permute-start | bytes 1597448 | tf_op jit(solution)/shard_map/ppermute | solution.py:52
  52.4 7.6 %collective-permute-start.19 = (bf16[1024,128]{1,0:T(8,128)(2,1)S(1)}, bf16[1024,128]{1,0:T(8,128)(2,1)S(1)}, u32[]{:S(2)}, u32[]{:S(2)}) collective-permute-start(bf16[1024,128]{1,0:T(8,128)(2,1)S(1)} %collective-permute-done.18.refs_9_), channel_id=1, source_target_pairs={{0,4},{4,8},{8,12},{12,16},{16,20},{20,24},{24,28},{28,0},{1,5},{5... | collective-permute-start | bytes 786440 | tf_op jit(solution)/shard_map/ppermute | solution.py:43
  53.5 7.6 %collective-permute-start.15 = (bf16[1024,128]{1,0:T(8,128)(2,1)S(1)}, bf16[1024,128]{1,0:T(8,128)(2,1)S(1)}, u32[]{:S(2)}, u32[]{:S(2)}) collective-permute-start(bf16[1024,128]{1,0:T(8,128)(2,1)S(1)} %collective-permute-done.14.refs_8_), channel_id=1, source_target_pairs={{0,28},{4,0},{8,4},{12,8},{16,12},{20,16},{24,20},{28,24},{1,29},{... | collective-permute-start | bytes 786440 | tf_op jit(solution)/shard_map/ppermute | solution.py:43
  60.0 9.3 %collective-permute-start.24 = (bf16[2080,128]{1,0:T(8,128)(2,1)S(1)}, bf16[2080,128]{1,0:T(8,128)(2,1)S(1)}, u32[]{:S(2)}, u32[]{:S(2)}) collective-permute-start(bf16[2080,128]{1,0:T(8,128)(2,1)S(1)} %pad_maximum_fusion.refs_14_), channel_id=1, source_target_pairs={{0,64},{32,96},{64,128},{96,160},{128,192},{160,224},{192,0},{224,... | collective-permute-start | bytes 1597448 | tf_op jit(solution)/shard_map/ppermute | solution.py:52
  60.3 14.0 %collective-permute-start.20 = (bf16[2112,128]{1,0:T(8,128)(2,1)S(1)}, bf16[2112,128]{1,0:T(8,128)(2,1)S(1)}, u32[]{:S(2)}, u32[]{:S(2)}) collective-permute-start(bf16[2112,128]{1,0:T(8,128)(2,1)S(1)} %slice.29), channel_id=1, source_target_pairs={{0,1},{1,2},{2,3},{3,0},{4,5},{5,6},{6,7},{7,4},{8,9},{9,10},{10,1... | collective-permute-start | bytes 1622024 | tf_op jit(solution)/shard_map/ppermute | solution.py:47
  61.1 13.1 %collective-permute-start.16 = (bf16[2112,128]{1,0:T(8,128)(2,1)S(1)}, bf16[2112,128]{1,0:T(8,128)(2,1)S(1)}, u32[]{:S(2)}, u32[]{:S(2)}) collective-permute-start(bf16[2112,128]{1,0:T(8,128)(2,1)S(1)} %slice.28), channel_id=1, source_target_pairs={{0,3},{1,0},{2,1},{3,2},{4,7},{5,4},{6,5},{7,6},{8,11},{9,8},{10,9... | collective-permute-start | bytes 1622024 | tf_op jit(solution)/shard_map/ppermute | solution.py:47
  63.7 10.5 %collective-permute-start.25 = (bf16[2080,128]{1,0:T(8,128)(2,1)S(1)}, bf16[2080,128]{1,0:T(8,128)(2,1)S(1)}, u32[]{:S(2)}, u32[]{:S(2)}) collective-permute-start(bf16[2080,128]{1,0:T(8,128)(2,1)S(1)} %collective-permute-done.23.refs_15_), channel_id=1, source_target_pairs={{0,192},{32,224},{64,0},{96,32},{128,64},{160,96},{192,128},{224,1... | collective-permute-start | bytes 1597448 | tf_op jit(solution)/shard_map/ppermute | solution.py:52
  65.5 6.3 %collective-permute-start.22 = (bf16[512,128]{1,0:T(8,128)(2,1)S(1)}, bf16[512,128]{1,0:T(8,128)(2,1)S(1)}, u32[]{:S(2)}, u32[]{:S(2)}) collective-permute-start(bf16[512,128]{1,0:T(8,128)(2,1)S(1)} %slice.33), channel_id=1, source_target_pairs={{0,4},{4,8},{8,12},{12,16},{16,20},{20,24},{24,28},{28,0},{1,5},{5... | collective-permute-start | bytes 393224 | tf_op jit(solution)/shard_map/ppermute | solution.py:43
  (3 other events, 24.5 us)

commit v3 on v2

--- a/solution.py
+++ b/solution.py
@@ -63,8 +63,8 @@
 
 def kernel(n_a, *refs):
     a_parts, refs = refs[:n_a], refs[n_a:]
-    b_parts, refs = refs[:-11], refs[-11:]
-    o_hbm, out, a_ref, b_ref, u_at, v_at, live, work, info, sinfo, sem = refs
+    b_parts, refs = refs[:-12], refs[-12:]
+    o_hbm, out, a_ref, b_ref, u_at, v_at, live, work, work_high, info, sinfo, sem = refs
     loads = []
     for slot, (parts, whole) in enumerate(((b_parts, b_ref), (a_parts, a_ref))):
         row = 0
@@ -84,7 +84,7 @@
         out[i] = jnp.zeros((BS, CS * BS), jnp.float32)
         return carry
 
-    lax.fori_loop(0, RB + 1, clear, 0)
+    lax.fori_loop(0, RB // 2, clear, 0)
     for load in loads:
         load.wait()
 
@@ -94,6 +94,7 @@
         info[i : i + 1, :] = (tile[0:1] * 64 + tile[1:2]).astype(jnp.int32)
     to_scalar = pltpu.make_async_copy(info, sinfo, sem.at[2])
     to_scalar.start()
+    lax.fori_loop(RB // 2, RB + 1, clear, 0)
     to_scalar.wait()
 
     def found(i, n):
@@ -103,7 +104,8 @@
             n = n + jnp.where((v & 63) < CS, 1, 0)
         return n
 
-    def listed(i, n):
+    def listed(i, carry):
+        n, n_high = carry
         b = live[i]
         k, b = b >> 12, b & 0xFFF
         piece, low = u_at[k & (CHUNKS - 1)], v_at[k & (CHUNKS - 1)]
@@ -111,31 +113,42 @@
         low = (low << 17) + b
         for s in range(SA):
             x = sinfo[piece, s] ^ k
-            work[n] = (top + (s * BS << 13) if s * BS < CUT else low + (s * BS - CUT << 13)) + (x << 6)
-            n = n + jnp.where((x & ~((RB - 1) << 6)) == 0, 1, 0)
-        return n
-
-    n = lax.fori_loop(0, lax.fori_loop(0, PARTS, found, jnp.int32(0)), listed, jnp.int32(0))
+            word = (top + (s * BS << 13) if s * BS < CUT else low + (s * BS - CUT << 13)) + (x << 6)
+            work[n] = word
+            work_high[n_high] = word
+            n = n + jnp.where((x & ~((RB // 2 - 1) << 6)) == 0, 1, 0)
+            n_high = n_high + jnp.where(x - ((RB // 2) << 6) == (x & ((RB // 2 - 1) << 6)), 1, 0)
+        return n, n_high
+
+    count = lax.fori_loop(0, PARTS, found, jnp.int32(0))
+    n, n_high = lax.fori_loop(0, count, listed, (jnp.int32(0), jnp.int32(0)))
     for g in range(GROUP):
         work[n + g] = RB << 12
-
-    def products(i, carry):
-        words = [work[i * GROUP + g] for g in range(GROUP)]
-        results = []
-        for w in words:
-            a = a_ref[pl.ds(pl.multiple_of((w >> 17) * 16, 16), BS), :]
-            b = b_ref[pl.ds(pl.multiple_of(((w >> 2) & 0x3FF) * 16, 16), BS), :]
-            results.append(jnp.dot(a, b, preferred_element_type=jnp.float32))
-        for w, result in zip(words, results):
-            out[(w >> 12) & 31, :, pl.ds(pl.multiple_of((w & 3) * BS, BS), BS)] += result
-        return carry
-
-    lax.fori_loop(0, (n + GROUP - 1) // GROUP, products, 0)
+        work_high[n_high + g] = RB << 12
+
+    def products(words, count):
+        def step(i, carry):
+            group = [words[i * GROUP + g] for g in range(GROUP)]
+            results = []
+            for w in group:
+                a = a_ref[pl.ds(pl.multiple_of((w >> 17) * 16, 16), BS), :]
+                b = b_ref[pl.ds(pl.multiple_of(((w >> 2) & 0x3FF) * 16, 16), BS), :]
+                results.append(jnp.dot(a, b, preferred_element_type=jnp.float32))
+            for w, result in zip(group, results):
+                out[(w >> 12) & 31, :, pl.ds(pl.multiple_of((w & 3) * BS, BS), BS)] += result
+            return carry
+
+        lax.fori_loop(0, (count + GROUP - 1) // GROUP, step, 0)
+
+    half = RB // 2
     stores = [
-        pltpu.make_async_copy(out.at[pl.ds(r, 4)], o_hbm.at[pl.ds(r, 4)], sem.at[3]) for r in range(0, RB, 4)
+        pltpu.make_async_copy(out.at[pl.ds(r, half)], o_hbm.at[pl.ds(r, half)], sem.at[3 + i])
+        for i, r in enumerate((0, half))
     ]
-    for store in stores:
-        store.start()
+    products(work, n)
+    stores[0].start()
+    products(work_high, n_high)
+    stores[1].start()
     for store in stores:
         store.wait()
 
@@ -155,9 +168,10 @@
             pltpu.SMEM((CHUNKS,), jnp.int32),
             pltpu.SMEM((PARTS * SB + 1,), jnp.int32),
             pltpu.SMEM((LIST,), jnp.int32),
+            pltpu.SMEM((LIST,), jnp.int32),
             pltpu.VMEM((CHUNKS + PARTS, BS), jnp.int32),
             pltpu.SMEM((CHUNKS + PARTS, BS), jnp.int32),
-            pltpu.SemaphoreType.DMA((4,)),
+            pltpu.SemaphoreType.DMA((5,)),
         ],
         compiler_params=pltpu.CompilerParams(vmem_limit_bytes=20 * 2**20),
         cost_estimate=pl.CostEstimate(flops=10**9, bytes_accessed=13 * 10**6, transcendentals=0),
@@ -176,12 +190,12 @@
     u2, um2 = along_z(u1, -1), along_z(um1, 1)
     by1 = along_y(after(b, u1), -1)
     v2 = along_x(v1, -1)
-    u3, um3 = along_z(u2, -1), along_z(um2, 1)
-    bm1 = along_y(after(b, u2), 1)
+    u3, um3 = along_z(after(u2, v1), -1), along_z(after(um2, vm1), 1)
     w = after(cat([v, v1, vm1, v2]), u3, um3)
     u4 = along_z(u3, -1)
+    bm1 = along_y(after(b, u4), 1)
     w1, wm1 = along_z(w, -1), along_z(w, 1)
-    x = cat([u, u1, um1, u2, um2, u3, um3, u4])
+    x = after(cat([u, u1, um1, u2, um2, u3, um3, u4]), v2, by1)
     xp, xm = along_x(x, -1), along_x(x, 1)
     w2, wm2 = along_z(w1, -1), along_z(wm1, 1)
     by2 = along_y(after(by1, w1), -1)
@@ -189,7 +203,7 @@
     half = NZ // 2 * UR
     xh0, xh1 = along_x(after(xp, w3)[:half], -1), along_x(after(xm, wm3)[half:], 1)
     half = NX // 2 * VR
-    wh0, wh1 = along_z(w3[:half], -1), along_z(wm3[half:], 1)
+    wh0, wh1 = along_z(after(w3, bm1)[:half], -1), along_z(after(wm3, bm1)[half:], 1)
 
     a_parts = [x, xp, xm, xh0, xh1, w, w1, wm1, w2, wm2, w3, wm3, wh0, wh1]
     return multiply(a_parts, [b, by1, bm1, by2]).reshape(RB * BS, CS * BS)

time: 83 us -> 83 us (level)
  waiting for transfers between devices: 27.4 us -> 29 us
  starting transfers between devices: 42.2 us -> 41.2 us
    ppermute x15, waiting for transfers between devices: 23.8 us -> 17.9 us  [along_z(): return lax.ppermute(x, 'col', [(i, (i + d) % NZ) for i in range(NZ)])]
    ppermute x3, waiting for transfers between devices: 3.64 us -> 7.95 us  [along_y(): return lax.ppermute(x, 'row', [(i, (i + 2 * d) % n) for i in range(n)])]
    ppermute x7, waiting for transfers between devices: 0.02 us -> 3.11 us  [along_x(): return lax.ppermute(x, 'layer', [(i, (i + d) % NX) for i in range(NX)])]
    ppermute x7, starting transfers between devices: 12.6 us -> 11.7 us  [along_x(): return lax.ppermute(x, 'layer', [(i, (i + d) % NX) for i in range(NX)])]
  transfers between devices with their start and end apart: 26 -> 26, of which waited for: 9 -> 11; matrix products, arithmetic and copies ran while one was open for 3% -> 3% of each run, Pallas kernels for 0% -> 0%
where the time goes in v3:
time: 83 us; the launch traced here: 82.2 us
  starting transfers between devices  41.2 us (50%)
  waiting for transfers between devices  29 us (35%)
  Pallas kernels  7.29 us (9%)
  other arithmetic  2.45 us (3%)
  local copies, waits for them, and re-layouts  2.02 us (2%)
    ppermute x15, starting transfers between devices, along_z(): return lax.ppermute(x, 'col', [(i, (i + d) % NZ) for i in range(NZ)])  26.1 us
    ppermute x15, waiting for transfers between devices, along_z(): return lax.ppermute(x, 'col', [(i, (i + d) % NZ) for i in range(NZ)])  17.9 us
    ppermute x7, starting transfers between devices, along_x(): return lax.ppermute(x, 'layer', [(i, (i + d) % NX) for i in range(NX)])  11.7 us
    ppermute x3, waiting for transfers between devices, along_y(): return lax.ppermute(x, 'row', [(i, (i + 2 * d) % n) for i in range(n)])  7.95 us
    pallas_call x1, Pallas kernels, multiply(): pl.pallas_call(functools.partial(kernel, len(a_parts)), out_shape=jax.Sha...  7.29 us
    ppermute x3, starting transfers between devices, along_y(): return lax.ppermute(x, 'row', [(i, (i + 2 * d) % n) for i in range(n)])  3.36 us
    ppermute x7, waiting for transfers between devices, along_x(): return lax.ppermute(x, 'layer', [(i, (i + d) % NX) for i in range(NX)])  3.11 us
  transfers between devices with their start and end apart: 26, of which 11 were waited for; matrix products, arithmetic and copies ran while one was open for 3% of the time, Pallas kernels for 0%

profile of v3, /device:TPU:24, one launch (start us, length us, event | category | flops | bytes accessed | tf_op | source)
XLA Modules:
  0.0 82.2 jit_solution(7409912032632861189)
XLA Ops:
  3.4 2.0 %collective-permute-start.1 = (bf16[528,128]{1,0:T(8,128)(2,1)S(1)}, bf16[528,128]{1,0:T(8,128)(2,1)S(1)}, u32[]{:S(2)}, u32[]{:S(2)}) collective-permute-start(bf16[528,128]{1,0:T(8,128)(2,1)S(1)} %pad_maximum_fusion.3), channel_id=1, source_target_pairs={{0,4},{4,8},{8,12},{12,16},{16,20},{20,24},{24,28},{28,0},{1,5},{5... | collective-permute-start | bytes 405512 | tf_op jit(solution)/shard_map/ppermute | solution.py:43
  5.4 4.0 %collective-permute-start = (bf16[528,128]{1,0:T(8,128)(2,1)S(1)}, bf16[528,128]{1,0:T(8,128)(2,1)S(1)}, u32[]{:S(2)}, u32[]{:S(2)}) collective-permute-start(bf16[528,128]{1,0:T(8,128)(2,1)S(1)} %pad_maximum_fusion.3), channel_id=1, source_target_pairs={{0,28},{4,0},{8,4},{12,8},{16,12},{20,16},{24,20},{28,24},{1,29},{... | collective-permute-start | bytes 405512 | tf_op jit(solution)/shard_map/ppermute | solution.py:43
  10.3 3.3 %collective-permute-done.1 = bf16[528,128]{1,0:T(8,128)(2,1)S(1)} collective-permute-done((bf16[528,128]{1,0:T(8,128)(2,1)S(1)}, bf16[528,128]{1,0:T(8,128)(2,1)S(1)}, u32[]{:S(2)}, u32[]{:S(2)}) %collective-permute-start.1) | collective-permute-done | bytes 135200 | tf_op jit(solution)/shard_map/ppermute | solution.py:43
  13.6 3.2 %collective-permute-start.2 = (bf16[528,128]{1,0:T(8,128)(2,1)S(1)}, bf16[528,128]{1,0:T(8,128)(2,1)S(1)}, u32[]{:S(2)}, u32[]{:S(2)}) collective-permute-start(bf16[528,128]{1,0:T(8,128)(2,1)S(1)} %collective-permute-done), channel_id=1, source_target_pairs={{0,28},{4,0},{8,4},{12,8},{16,12},{20,16},{24,20},{28,24},{1,29},{... | collective-permute-start | bytes 405512 | tf_op jit(solution)/shard_map/ppermute | solution.py:43
  16.9 2.8 %collective-permute-start.5 = (bf16[256,128]{1,0:T(8,128)(2,1)S(1)}, bf16[256,128]{1,0:T(8,128)(2,1)S(1)}, u32[]{:S(2)}, u32[]{:S(2)}) collective-permute-start(bf16[256,128]{1,0:T(8,128)(2,1)S(1)} %bitcast.12), channel_id=1, source_target_pairs={{0,3},{1,0},{2,1},{3,2},{4,7},{5,4},{6,5},{7,6},{8,11},{9,8},{10,9... | collective-permute-start | bytes 196616 | tf_op jit(solution)/shard_map/ppermute | solution.py:47
  21.7 1.5 %collective-permute-start.6 = (bf16[528,128]{1,0:T(8,128)(2,1)S(1)}, bf16[528,128]{1,0:T(8,128)(2,1)S(1)}, u32[]{:S(2)}, u32[]{:S(2)}) collective-permute-start(bf16[528,128]{1,0:T(8,128)(2,1)S(1)} %collective-permute-done.2), channel_id=1, source_target_pairs={{0,28},{4,0},{8,4},{12,8},{16,12},{20,16},{24,20},{28,24},{1,29},{... | collective-permute-start | bytes 405512 | tf_op jit(solution)/shard_map/ppermute | solution.py:43
  23.2 2.1 %collective-permute-done.7 = bf16[256,128]{1,0:T(8,128)(2,1)S(1)} collective-permute-done((bf16[256,128]{1,0:T(8,128)(2,1)S(1)}, bf16[256,128]{1,0:T(8,128)(2,1)S(1)}, u32[]{:S(2)}, u32[]{:S(2)}) %collective-permute-start.7) | collective-permute-done | bytes 65568 | tf_op jit(solution)/shard_map/ppermute | solution.py:47
  25.4 2.1 %collective-permute-start.10 = (bf16[256,128]{1,0:T(8,128)(2,1)S(1)}, bf16[256,128]{1,0:T(8,128)(2,1)S(1)}, u32[]{:S(2)}, u32[]{:S(2)}) collective-permute-start(bf16[256,128]{1,0:T(8,128)(2,1)S(1)} %collective-permute-done.5), channel_id=1, source_target_pairs={{0,3},{1,0},{2,1},{3,2},{4,7},{5,4},{6,5},{7,6},{8,11},{9,8},{10,9... | collective-permute-start | bytes 196616 | tf_op jit(solution)/shard_map/ppermute | solution.py:47
  27.5 1.9 %collective-permute-start.9 = (bf16[528,128]{1,0:T(8,128)(2,1)S(1)}, bf16[528,128]{1,0:T(8,128)(2,1)S(1)}, u32[]{:S(2)}, u32[]{:S(2)}) collective-permute-start(bf16[528,128]{1,0:T(8,128)(2,1)S(1)} %collective-permute-done.6), channel_id=1, source_target_pairs={{0,28},{4,0},{8,4},{12,8},{16,12},{20,16},{24,20},{28,24},{1,29},{... | collective-permute-start | bytes 405512 | tf_op jit(solution)/shard_map/ppermute | solution.py:43
  29.4 2.1 %collective-permute-done.8 = bf16[528,128]{1,0:T(8,128)(2,1)S(1)} collective-permute-done((bf16[528,128]{1,0:T(8,128)(2,1)S(1)}, bf16[528,128]{1,0:T(8,128)(2,1)S(1)}, u32[]{:S(2)}, u32[]{:S(2)}) %collective-permute-start.8) | collective-permute-done | bytes 135200 | tf_op jit(solution)/shard_map/ppermute | solution.py:43
  32.6 1.7 %collective-permute-done.11.refs_15_ = bf16[2080,128]{1,0:T(8,128)(2,1)S(1)} collective-permute-done((bf16[2080,128]{1,0:T(8,128)(2,1)S(1)}, bf16[2080,128]{1,0:T(8,128)(2,1)S(1)}, u32[]{:S(2)}, u32[]{:S(2)}) %collective-permute-start.11) | collective-permute-done | bytes 532512 | tf_op jit(solution)/shard_map/ppermute | solution.py:52
  34.7 2.8 %collective-permute-start.12 = (bf16[4224,128]{1,0:T(8,128)(2,1)S(1)}, bf16[4224,128]{1,0:T(8,128)(2,1)S(1)}, u32[]{:S(2)}, u32[]{:S(2)}) collective-permute-start(bf16[4224,128]{1,0:T(8,128)(2,1)S(1)} %constant_dynamic-update-slice_fusion.refs_0_), channel_id=1, source_target_pairs={{0,3},{1,0},{2,1},{3,2},{4,7},{5,4},{6,5},{7,6},{8,11},{9,8},{10,9... | collective-permute-start | bytes 3244040 | tf_op jit(solution)/shard_map/ppermute | solution.py:47
  37.6 3.2 %collective-permute-start.14 = (bf16[1024,128]{1,0:T(8,128)(2,1)S(1)}, bf16[1024,128]{1,0:T(8,128)(2,1)S(1)}, u32[]{:S(2)}, u32[]{:S(2)}) collective-permute-start(bf16[1024,128]{1,0:T(8,128)(2,1)S(1)} %pad_maximum_fusion.2.refs_5_), channel_id=1, source_target_pairs={{0,28},{4,0},{8,4},{12,8},{16,12},{20,16},{24,20},{28,24},{1,29},{... | collective-permute-start | bytes 786440 | tf_op jit(solution)/shard_map/ppermute | solution.py:43
  40.8 4.3 %collective-permute-done.18.refs_7_ = bf16[1024,128]{1,0:T(8,128)(2,1)S(1)} collective-permute-done((bf16[1024,128]{1,0:T(8,128)(2,1)S(1)}, bf16[1024,128]{1,0:T(8,128)(2,1)S(1)}, u32[]{:S(2)}, u32[]{:S(2)}) %collective-permute-start.18) | collective-permute-done | bytes 262176 | tf_op jit(solution)/shard_map/ppermute | solution.py:43
  45.2 3.2 %collective-permute-start.15 = (bf16[1024,128]{1,0:T(8,128)(2,1)S(1)}, bf16[1024,128]{1,0:T(8,128)(2,1)S(1)}, u32[]{:S(2)}, u32[]{:S(2)}) collective-permute-start(bf16[1024,128]{1,0:T(8,128)(2,1)S(1)} %collective-permute-done.14.refs_6_), channel_id=1, source_target_pairs={{0,28},{4,0},{8,4},{12,8},{16,12},{20,16},{24,20},{28,24},{1,29},{... | collective-permute-start | bytes 786440 | tf_op jit(solution)/shard_map/ppermute | solution.py:43
  48.4 4.6 %collective-permute-done.19.refs_9_ = bf16[1024,128]{1,0:T(8,128)(2,1)S(1)} collective-permute-done((bf16[1024,128]{1,0:T(8,128)(2,1)S(1)}, bf16[1024,128]{1,0:T(8,128)(2,1)S(1)}, u32[]{:S(2)}, u32[]{:S(2)}) %collective-permute-start.19) | collective-permute-done | bytes 262176 | tf_op jit(solution)/shard_map/ppermute | solution.py:43
  53.7 2.8 %collective-permute-start.16 = (bf16[1024,128]{1,0:T(8,128)(2,1)S(1)}, bf16[1024,128]{1,0:T(8,128)(2,1)S(1)}, u32[]{:S(2)}, u32[]{:S(2)}) collective-permute-start(bf16[1024,128]{1,0:T(8,128)(2,1)S(1)} %collective-permute-done.15.refs_8_), channel_id=1, source_target_pairs={{0,28},{4,0},{8,4},{12,8},{16,12},{20,16},{24,20},{28,24},{1,29},{... | collective-permute-start | bytes 786440 | tf_op jit(solution)/shard_map/ppermute | solution.py:43
  56.5 1.4 %collective-permute-start.22 = (bf16[2080,128]{1,0:T(8,128)(2,1)S(1)}, bf16[2080,128]{1,0:T(8,128)(2,1)S(1)}, u32[]{:S(2)}, u32[]{:S(2)}) collective-permute-start(bf16[2080,128]{1,0:T(8,128)(2,1)S(1)} %pad_maximum_fusion.refs_14_), channel_id=1, source_target_pairs={{0,64},{32,96},{64,128},{96,160},{128,192},{160,224},{192,0},{224,... | collective-permute-start | bytes 1597448 | tf_op jit(solution)/shard_map/ppermute | solution.py:52
  58.0 2.6 %collective-permute-done.20.refs_11_ = bf16[1024,128]{1,0:T(8,128)(2,1)S(1)} collective-permute-done((bf16[1024,128]{1,0:T(8,128)(2,1)S(1)}, bf16[1024,128]{1,0:T(8,128)(2,1)S(1)}, u32[]{:S(2)}, u32[]{:S(2)}) %collective-permute-start.20) | collective-permute-done | bytes 262176 | tf_op jit(solution)/shard_map/ppermute | solution.py:43
  61.1 3.0 %collective-permute-start.17 = (bf16[2112,128]{1,0:T(8,128)(2,1)S(1)}, bf16[2112,128]{1,0:T(8,128)(2,1)S(1)}, u32[]{:S(2)}, u32[]{:S(2)}) collective-permute-start(bf16[2112,128]{1,0:T(8,128)(2,1)S(1)} %slice.28), channel_id=1, source_target_pairs={{0,3},{1,0},{2,1},{3,2},{4,7},{5,4},{6,5},{7,6},{8,11},{9,8},{10,9... | collective-permute-start | bytes 1622024 | tf_op jit(solution)/shard_map/ppermute | solution.py:47
  65.8 1.9 %collective-permute-start.24 = (bf16[512,128]{1,0:T(8,128)(2,1)S(1)}, bf16[512,128]{1,0:T(8,128)(2,1)S(1)}, u32[]{:S(2)}, u32[]{:S(2)}) collective-permute-start(bf16[512,128]{1,0:T(8,128)(2,1)S(1)} %slice.31), channel_id=1, source_target_pairs={{0,4},{4,8},{8,12},{12,16},{16,20},{20,24},{24,28},{28,0},{1,5},{5... | collective-permute-start | bytes 393224 | tf_op jit(solution)/shard_map/ppermute | solution.py:43
  67.7 1.4 %collective-permute-start.23 = (bf16[512,128]{1,0:T(8,128)(2,1)S(1)}, bf16[512,128]{1,0:T(8,128)(2,1)S(1)}, u32[]{:S(2)}, u32[]{:S(2)}) collective-permute-start(bf16[512,128]{1,0:T(8,128)(2,1)S(1)} %slice.30), channel_id=1, source_target_pairs={{0,28},{4,0},{8,4},{12,8},{16,12},{20,16},{24,20},{28,24},{1,29},{... | collective-permute-start | bytes 393224 | tf_op jit(solution)/shard_map/ppermute | solution.py:43
  69.1 5.6 %collective-permute-done.25.refs_17_ = bf16[2080,128]{1,0:T(8,128)(2,1)S(1)} collective-permute-done((bf16[2080,128]{1,0:T(8,128)(2,1)S(1)}, bf16[2080,128]{1,0:T(8,128)(2,1)S(1)}, u32[]{:S(2)}, u32[]{:S(2)}) %collective-permute-start.25) | collective-permute-done | bytes 532512 | tf_op jit(solution)/shard_map/ppermute | solution.py:52
  74.8 7.3 %shard_map.46 = f32[16,128,512]{2,1,0:T(8,128)} custom-call(bf16[4224,128]{1,0:T(8,128)(2,1)S(1)} %constant_dynamic-update-slice_fusion.refs_0_, bf16[4224,128]{1,0:T(8,128)(2,1)S(1)} %collective-permute-done.12.refs_1_, bf16[4224,128]{1,0:T(8,128)(2,1)S(1)} %collective-permute-done.13.refs_2_, bf16[2112,128]{1,0:T(8,128)(2,1)S(1)} %collective-permute-done.17.refs_3_, ...), custom_call_target="tpu_custom_call" | custom-call | flops 1000000000 | bytes 13000000 | tf_op jit(solution)/shard_map/pallas_call | solution.py:158
  (53 shorter events, 10.7 us)
Async XLA Ops:
  1.7 15.2 %collective-permute-start.4 = (bf16[1040,128]{1,0:T(8,128)(2,1)S(1)}, bf16[1040,128]{1,0:T(8,128)(2,1)S(1)}, u32[]{:S(2)}, u32[]{:S(2)}) collective-permute-start(bf16[1040,128]{1,0:T(8,128)(2,1)S(1)} %pad_maximum_fusion.1), channel_id=1, source_target_pairs={{0,32},{32,0},{64,96},{96,64},{128,160},{160,128},{192,224},{224,1... | collective-permute-start | bytes 798728 | tf_op jit(solution)/shard_map/ppermute | solution.py:56
  3.4 10.2 %collective-permute-start.1 = (bf16[528,128]{1,0:T(8,128)(2,1)S(1)}, bf16[528,128]{1,0:T(8,128)(2,1)S(1)}, u32[]{:S(2)}, u32[]{:S(2)}) collective-permute-start(bf16[528,128]{1,0:T(8,128)(2,1)S(1)} %pad_maximum_fusion.3), channel_id=1, source_target_pairs={{0,4},{4,8},{8,12},{12,16},{16,20},{20,24},{24,28},{28,0},{1,5},{5... | collective-permute-start | bytes 405512 | tf_op jit(solution)/shard_map/ppermute | solution.py:43
  5.4 8.2 %collective-permute-start = (bf16[528,128]{1,0:T(8,128)(2,1)S(1)}, bf16[528,128]{1,0:T(8,128)(2,1)S(1)}, u32[]{:S(2)}, u32[]{:S(2)}) collective-permute-start(bf16[528,128]{1,0:T(8,128)(2,1)S(1)} %pad_maximum_fusion.3), channel_id=1, source_target_pairs={{0,28},{4,0},{8,4},{12,8},{16,12},{20,16},{24,20},{28,24},{1,29},{... | collective-permute-start | bytes 405512 | tf_op jit(solution)/shard_map/ppermute | solution.py:43
  13.6 9.6 %collective-permute-start.3 = (bf16[528,128]{1,0:T(8,128)(2,1)S(1)}, bf16[528,128]{1,0:T(8,128)(2,1)S(1)}, u32[]{:S(2)}, u32[]{:S(2)}) collective-permute-start(bf16[528,128]{1,0:T(8,128)(2,1)S(1)} %collective-permute-done.1), channel_id=1, source_target_pairs={{0,4},{4,8},{8,12},{12,16},{16,20},{20,24},{24,28},{28,0},{1,5},{5... | collective-permute-start | bytes 405512 | tf_op jit(solution)/shard_map/ppermute | solution.py:43
  13.6 7.1 %collective-permute-start.2 = (bf16[528,128]{1,0:T(8,128)(2,1)S(1)}, bf16[528,128]{1,0:T(8,128)(2,1)S(1)}, u32[]{:S(2)}, u32[]{:S(2)}) collective-permute-start(bf16[528,128]{1,0:T(8,128)(2,1)S(1)} %collective-permute-done), channel_id=1, source_target_pairs={{0,28},{4,0},{8,4},{12,8},{16,12},{20,16},{24,20},{28,24},{1,29},{... | collective-permute-start | bytes 405512 | tf_op jit(solution)/shard_map/ppermute | solution.py:43
  19.8 5.6 %collective-permute-start.7 = (bf16[256,128]{1,0:T(8,128)(2,1)S(1)}, bf16[256,128]{1,0:T(8,128)(2,1)S(1)}, u32[]{:S(2)}, u32[]{:S(2)}) collective-permute-start(bf16[256,128]{1,0:T(8,128)(2,1)S(1)} %bitcast.13), channel_id=1, source_target_pairs={{0,1},{1,2},{2,3},{3,0},{4,5},{5,6},{6,7},{7,4},{8,9},{9,10},{10,1... | collective-permute-start | bytes 196616 | tf_op jit(solution)/shard_map/ppermute | solution.py:47
  19.9 14.4 %collective-permute-start.11 = (bf16[2080,128]{1,0:T(8,128)(2,1)S(1)}, bf16[2080,128]{1,0:T(8,128)(2,1)S(1)}, u32[]{:S(2)}, u32[]{:S(2)}) collective-permute-start(bf16[2080,128]{1,0:T(8,128)(2,1)S(1)} %pad_maximum_fusion.refs_14_), channel_id=1, source_target_pairs={{0,192},{32,224},{64,0},{96,32},{128,64},{160,96},{192,128},{224,1... | collective-permute-start | bytes 1597448 | tf_op jit(solution)/shard_map/ppermute | solution.py:52
  21.7 5.8 %collective-permute-start.6 = (bf16[528,128]{1,0:T(8,128)(2,1)S(1)}, bf16[528,128]{1,0:T(8,128)(2,1)S(1)}, u32[]{:S(2)}, u32[]{:S(2)}) collective-permute-start(bf16[528,128]{1,0:T(8,128)(2,1)S(1)} %collective-permute-done.2), channel_id=1, source_target_pairs={{0,28},{4,0},{8,4},{12,8},{16,12},{20,16},{24,20},{28,24},{1,29},{... | collective-permute-start | bytes 405512 | tf_op jit(solution)/shard_map/ppermute | solution.py:43
  25.4 6.2 %collective-permute-start.8 = (bf16[528,128]{1,0:T(8,128)(2,1)S(1)}, bf16[528,128]{1,0:T(8,128)(2,1)S(1)}, u32[]{:S(2)}, u32[]{:S(2)}) collective-permute-start(bf16[528,128]{1,0:T(8,128)(2,1)S(1)} %collective-permute-done.3), channel_id=1, source_target_pairs={{0,4},{4,8},{8,12},{12,16},{16,20},{20,24},{24,28},{28,0},{1,5},{5... | collective-permute-start | bytes 405512 | tf_op jit(solution)/shard_map/ppermute | solution.py:43
  25.4 7.2 %collective-permute-start.10 = (bf16[256,128]{1,0:T(8,128)(2,1)S(1)}, bf16[256,128]{1,0:T(8,128)(2,1)S(1)}, u32[]{:S(2)}, u32[]{:S(2)}) collective-permute-start(bf16[256,128]{1,0:T(8,128)(2,1)S(1)} %collective-permute-done.5), channel_id=1, source_target_pairs={{0,3},{1,0},{2,1},{3,2},{4,7},{5,4},{6,5},{7,6},{8,11},{9,8},{10,9... | collective-permute-start | bytes 196616 | tf_op jit(solution)/shard_map/ppermute | solution.py:47
  34.3 26.3 %collective-permute-start.13 = (bf16[4224,128]{1,0:T(8,128)(2,1)S(1)}, bf16[4224,128]{1,0:T(8,128)(2,1)S(1)}, u32[]{:S(2)}, u32[]{:S(2)}) collective-permute-start(bf16[4224,128]{1,0:T(8,128)(2,1)S(1)} %constant_dynamic-update-slice_fusion.refs_0_), channel_id=1, source_target_pairs={{0,1},{1,2},{2,3},{3,0},{4,5},{5,6},{6,7},{7,4},{8,9},{9,10},{10,1... | collective-permute-start | bytes 3244040 | tf_op jit(solution)/shard_map/ppermute | solution.py:47
  34.7 26.4 %collective-permute-start.12 = (bf16[4224,128]{1,0:T(8,128)(2,1)S(1)}, bf16[4224,128]{1,0:T(8,128)(2,1)S(1)}, u32[]{:S(2)}, u32[]{:S(2)}) collective-permute-start(bf16[4224,128]{1,0:T(8,128)(2,1)S(1)} %constant_dynamic-update-slice_fusion.refs_0_), channel_id=1, source_target_pairs={{0,3},{1,0},{2,1},{3,2},{4,7},{5,4},{6,5},{7,6},{8,11},{9,8},{10,9... | collective-permute-start | bytes 3244040 | tf_op jit(solution)/shard_map/ppermute | solution.py:47
  37.5 7.7 %collective-permute-start.18 = (bf16[1024,128]{1,0:T(8,128)(2,1)S(1)}, bf16[1024,128]{1,0:T(8,128)(2,1)S(1)}, u32[]{:S(2)}, u32[]{:S(2)}) collective-permute-start(bf16[1024,128]{1,0:T(8,128)(2,1)S(1)} %pad_maximum_fusion.2.refs_5_), channel_id=1, source_target_pairs={{0,4},{4,8},{8,12},{12,16},{16,20},{20,24},{24,28},{28,0},{1,5},{5... | collective-permute-start | bytes 786440 | tf_op jit(solution)/shard_map/ppermute | solution.py:43
  37.6 7.6 %collective-permute-start.14 = (bf16[1024,128]{1,0:T(8,128)(2,1)S(1)}, bf16[1024,128]{1,0:T(8,128)(2,1)S(1)}, u32[]{:S(2)}, u32[]{:S(2)}) collective-permute-start(bf16[1024,128]{1,0:T(8,128)(2,1)S(1)} %pad_maximum_fusion.2.refs_5_), channel_id=1, source_target_pairs={{0,28},{4,0},{8,4},{12,8},{16,12},{20,16},{24,20},{28,24},{1,29},{... | collective-permute-start | bytes 786440 | tf_op jit(solution)/shard_map/ppermute | solution.py:43
  45.2 7.8 %collective-permute-start.19 = (bf16[1024,128]{1,0:T(8,128)(2,1)S(1)}, bf16[1024,128]{1,0:T(8,128)(2,1)S(1)}, u32[]{:S(2)}, u32[]{:S(2)}) collective-permute-start(bf16[1024,128]{1,0:T(8,128)(2,1)S(1)} %collective-permute-done.18.refs_7_), channel_id=1, source_target_pairs={{0,4},{4,8},{8,12},{12,16},{16,20},{20,24},{24,28},{28,0},{1,5},{5... | collective-permute-start | bytes 786440 | tf_op jit(solution)/shard_map/ppermute | solution.py:43
  45.2 8.5 %collective-permute-start.15 = (bf16[1024,128]{1,0:T(8,128)(2,1)S(1)}, bf16[1024,128]{1,0:T(8,128)(2,1)S(1)}, u32[]{:S(2)}, u32[]{:S(2)}) collective-permute-start(bf16[1024,128]{1,0:T(8,128)(2,1)S(1)} %collective-permute-done.14.refs_6_), channel_id=1, source_target_pairs={{0,28},{4,0},{8,4},{12,8},{16,12},{20,16},{24,20},{28,24},{1,29},{... | collective-permute-start | bytes 786440 | tf_op jit(solution)/shard_map/ppermute | solution.py:43
  53.0 7.6 %collective-permute-start.20 = (bf16[1024,128]{1,0:T(8,128)(2,1)S(1)}, bf16[1024,128]{1,0:T(8,128)(2,1)S(1)}, u32[]{:S(2)}, u32[]{:S(2)}) collective-permute-start(bf16[1024,128]{1,0:T(8,128)(2,1)S(1)} %collective-permute-done.19.refs_9_), channel_id=1, source_target_pairs={{0,4},{4,8},{8,12},{12,16},{16,20},{20,24},{24,28},{28,0},{1,5},{5... | collective-permute-start | bytes 786440 | tf_op jit(solution)/shard_map/ppermute | solution.py:43
  53.7 7.3 %collective-permute-start.16 = (bf16[1024,128]{1,0:T(8,128)(2,1)S(1)}, bf16[1024,128]{1,0:T(8,128)(2,1)S(1)}, u32[]{:S(2)}, u32[]{:S(2)}) collective-permute-start(bf16[1024,128]{1,0:T(8,128)(2,1)S(1)} %collective-permute-done.15.refs_8_), channel_id=1, source_target_pairs={{0,28},{4,0},{8,4},{12,8},{16,12},{20,16},{24,20},{28,24},{1,29},{... | collective-permute-start | bytes 786440 | tf_op jit(solution)/shard_map/ppermute | solution.py:43
  56.5 9.3 %collective-permute-start.22 = (bf16[2080,128]{1,0:T(8,128)(2,1)S(1)}, bf16[2080,128]{1,0:T(8,128)(2,1)S(1)}, u32[]{:S(2)}, u32[]{:S(2)}) collective-permute-start(bf16[2080,128]{1,0:T(8,128)(2,1)S(1)} %pad_maximum_fusion.refs_14_), channel_id=1, source_target_pairs={{0,64},{32,96},{64,128},{96,160},{128,192},{160,224},{192,0},{224,... | collective-permute-start | bytes 1597448 | tf_op jit(solution)/shard_map/ppermute | solution.py:52
  60.6 14.1 %collective-permute-start.21 = (bf16[2112,128]{1,0:T(8,128)(2,1)S(1)}, bf16[2112,128]{1,0:T(8,128)(2,1)S(1)}, u32[]{:S(2)}, u32[]{:S(2)}) collective-permute-start(bf16[2112,128]{1,0:T(8,128)(2,1)S(1)} %slice.29), channel_id=1, source_target_pairs={{0,1},{1,2},{2,3},{3,0},{4,5},{5,6},{6,7},{7,4},{8,9},{9,10},{10,1... | collective-permute-start | bytes 1622024 | tf_op jit(solution)/shard_map/ppermute | solution.py:47
  61.1 13.7 %collective-permute-start.17 = (bf16[2112,128]{1,0:T(8,128)(2,1)S(1)}, bf16[2112,128]{1,0:T(8,128)(2,1)S(1)}, u32[]{:S(2)}, u32[]{:S(2)}) collective-permute-start(bf16[2112,128]{1,0:T(8,128)(2,1)S(1)} %slice.28), channel_id=1, source_target_pairs={{0,3},{1,0},{2,1},{3,2},{4,7},{5,4},{6,5},{7,6},{8,11},{9,8},{10,9... | collective-permute-start | bytes 1622024 | tf_op jit(solution)/shard_map/ppermute | solution.py:47
  64.1 10.7 %collective-permute-start.25 = (bf16[2080,128]{1,0:T(8,128)(2,1)S(1)}, bf16[2080,128]{1,0:T(8,128)(2,1)S(1)}, u32[]{:S(2)}, u32[]{:S(2)}) collective-permute-start(bf16[2080,128]{1,0:T(8,128)(2,1)S(1)} %collective-permute-done.11.refs_15_), channel_id=1, source_target_pairs={{0,192},{32,224},{64,0},{96,32},{128,64},{160,96},{192,128},{224,1... | collective-permute-start | bytes 1597448 | tf_op jit(solution)/shard_map/ppermute | solution.py:52
  65.8 8.9 %collective-permute-start.24 = (bf16[512,128]{1,0:T(8,128)(2,1)S(1)}, bf16[512,128]{1,0:T(8,128)(2,1)S(1)}, u32[]{:S(2)}, u32[]{:S(2)}) collective-permute-start(bf16[512,128]{1,0:T(8,128)(2,1)S(1)} %slice.31), channel_id=1, source_target_pairs={{0,4},{4,8},{8,12},{12,16},{16,20},{20,24},{24,28},{28,0},{1,5},{5... | collective-permute-start | bytes 393224 | tf_op jit(solution)/shard_map/ppermute | solution.py:43
  67.7 7.0 %collective-permute-start.23 = (bf16[512,128]{1,0:T(8,128)(2,1)S(1)}, bf16[512,128]{1,0:T(8,128)(2,1)S(1)}, u32[]{:S(2)}, u32[]{:S(2)}) collective-permute-start(bf16[512,128]{1,0:T(8,128)(2,1)S(1)} %slice.30), channel_id=1, source_target_pairs={{0,28},{4,0},{8,4},{12,8},{16,12},{20,16},{24,20},{28,24},{1,29},{... | collective-permute-start | bytes 393224 | tf_op jit(solution)/shard_map/ppermute | solution.py:43
  (3 other events, 26.6 us)
